TPU v7x, 128 devices: a whole 4x4x4 slice. The times are simulated.
128 devices in a mesh: row: 16 (over z, x), col: 8 (over y, core).
Axes of the slice: x: 4, y: 4, z: 4, core: 2. Of those that a mesh axis runs over, the one named last changes fastest.
Arguments:
- pivot_rows: bfloat16 [8, 1024, 7168], P('col', None, 'row'), may hold values from -1.25 to 1.25
- pivot_order: int32 [8, 1024], P('col'), may hold values from 0 to 1023, each once within a row
- inverse_lower: bfloat16 [8, 1024, 1024], P('col'), as said below
- inverse_upper: bfloat16 [8, 1024, 1024], P('col'), as said below
- front_rows: bfloat16 [8, 64, 128, 8192], P('col', 'row'), may hold values from -6 to 6
- slot_block: int32 [8, 64], replicated, may hold values from -1 to 55, as said below
- parent_map: int32 [8, 56], replicated, may hold values from 0 to 63, as said below
- parent_init: bfloat16 [4, 8192, 8192], P(None, ('row', 'col')), may hold values from -6 to 6
Outputs:
- lower_blocks: bfloat16 [8, 64, 128, 1024], P('col', 'row')
- upper_panel: bfloat16 [8, 1024, 7168], P('col', None, 'row')
- assembled: bfloat16 [4, 8192, 8192], P(None, ('row', 'col'))
Inputs may be any that keep to these rules, and one draw needn't show every extreme that they name: `slot_block`: in each front every trailing row block 0 to 55 is held by exactly one slot and -1 marks an empty slot; slots r * 4 to (r + 1) * 4 - 1 of a front lie on index r of row; in each front some index of row has all 4 slots live. `parent_map`: the entries of one front are distinct. `inverse_lower`: unit lower triangular. `inverse_upper`: upper triangular with a positive diagonal.
All inputs are finite; a program needn't handle non-finite values.
Results may differ from a plain program's by a relative error of at most 0.0057.
Values may be sent and summed in bfloat16 or wider, within the bound.
A program may use at most 128 MiB of HBM per device.

v0:
```python
import jax
import jax.numpy as jnp
from jax import lax
from jax.sharding import PartitionSpec as P


def shards(
    pivot_rows,
    pivot_order,
    inverse_lower,
    inverse_upper,
    front_rows,
    slot_block,
    parent_map,
    parent_init,
):
    col_count = lax.axis_size("col")
    row_index = lax.axis_index("row")
    col_index = lax.axis_index("col")
    slot_count = front_rows.shape[1]
    block_rows = front_rows.shape[2]
    pivots = inverse_lower.shape[1]
    fronts = slot_block.shape[0]
    capacity = slot_block.shape[1]
    block_count = parent_map.shape[1]
    parents = parent_init.shape[0]
    piece_cols = parent_init.shape[1]
    parent_order = parent_init.shape[2]
    parent_blocks = parent_order // block_rows
    trail_width = block_count * block_rows
    pivot_list = pivot_order[0]
    positions = jnp.arange(pivots, dtype=jnp.int32)
    inverse_list = jnp.zeros((pivots,), jnp.int32).at[pivot_list].set(positions)
    lower_perm = jnp.take(inverse_lower[0], inverse_list, axis=1)
    upper_part = jnp.dot(lower_perm, pivot_rows[0], preferred_element_type=jnp.float32).astype(
        jnp.bfloat16
    )
    front_slots = lax.dynamic_index_in_dim(slot_block, col_index, 0, keepdims=False)
    own_slots = lax.dynamic_slice_in_dim(front_slots, row_index * slot_count, slot_count)
    slot_live = own_slots >= 0
    rows_flat = front_rows[0].reshape(slot_count * block_rows, pivots + trail_width)
    lower_factor = jnp.dot(
        rows_flat[:, :pivots], inverse_upper[0], preferred_element_type=jnp.float32
    )
    keep_rows = jnp.repeat(slot_live, block_rows)[:, None]
    lower_factor = jnp.where(keep_rows, lower_factor, 0.0).astype(jnp.bfloat16)
    trailing = rows_flat[:, pivots:]
    product = jnp.dot(
        lower_factor,
        lax.all_gather(upper_part, "row", axis=1, tiled=True),
        preferred_element_type=jnp.float32,
    )
    schur_rows = (trailing.astype(jnp.float32) - product).astype(jnp.bfloat16)
    own_map = lax.dynamic_index_in_dim(parent_map, col_index, 0, keepdims=False)
    block_ids = jnp.arange(block_count, dtype=jnp.int32)
    parent_ids = jnp.arange(parent_blocks, dtype=jnp.int32)
    matches = parent_ids[:, None] == own_map[None, :]
    source_block = jnp.where(
        matches.any(axis=1), jnp.sum(jnp.where(matches, block_ids[None, :], 0), axis=1), block_count
    )
    blocked = schur_rows.reshape(slot_count * block_rows, block_count, block_rows)
    spread = jnp.take(blocked, source_block, axis=1, mode="fill", fill_value=0)
    spread = spread.reshape(slot_count, block_rows, parent_order)
    position_lookup = jnp.arange(capacity, dtype=jnp.int32)
    holder = jnp.sum(
        jnp.where(
            slot_block[:, None, :] == block_ids[None, :, None], position_lookup[None, None, :], 0
        ),
        axis=2,
    )
    hits = parent_map[:, None, :] == parent_ids[None, :, None]
    present = hits.any(axis=2)
    child_block = jnp.sum(jnp.where(hits, block_ids[None, None, :], 0), axis=2)
    source_place = jnp.take_along_axis(holder, child_block, axis=1)
    source_row = source_place // slot_count
    source_slot = source_place % slot_count
    front_ids = jnp.arange(fronts, dtype=jnp.int32)[:, None]
    arrived = lax.all_to_all(spread, ("row", "col"), split_axis=2, concat_axis=0, tiled=True)
    item_index = (source_row * col_count + front_ids) * slot_count + source_slot
    item_total = arrived.shape[0]
    item_index = jnp.where(present, item_index, item_total)
    picked = jnp.take(arrived, item_index.reshape(-1), axis=0, mode="fill", fill_value=0)
    picked = picked.reshape(parents, 2, parent_blocks, block_rows, piece_cols)
    summed = picked[:, 0].astype(jnp.float32) + picked[:, 1].astype(jnp.float32)
    columns_first = jnp.transpose(summed, (0, 3, 1, 2)).reshape(parents, piece_cols, parent_order)
    assembled = (parent_init.astype(jnp.float32) + columns_first).astype(jnp.bfloat16)
    lower_out = lower_factor.reshape(1, slot_count, block_rows, pivots)
    return (lower_out, upper_part[None], assembled)


def solution(mesh):
    return jax.shard_map(
        shards,
        mesh=mesh,
        in_specs=(
            P("col", None, "row"),
            P("col", None),
            P("col", None, None),
            P("col", None, None),
            P("col", "row", None, None),
            P(),
            P(),
            P(None, ("row", "col"), None),
        ),
        out_specs=(
            P("col", "row", None, None),
            P("col", None, "row"),
            P(None, ("row", "col"), None),
        ),
        check_vma=False,
    )
```

profile of v0, /device:TPU:15, one launch (start us, length us, event | category | flops | bytes accessed | tf_op | source)
XLA Modules:
  0.0 380.7 jit_solution(11380906789137521319)
XLA Ops:
  7.2 0.0 copy-start
  7.2 0.0 all-gather.2.cloned.1.call-start
  7.2 0.8 compare_select_fusion
  8.1 4.3 %scatter_custom_fusion = s32[1024]{0:T(1024)S(1)} fusion(s32[1024]{0:T(1024)S(1)} %bitcast.67, s32[1024]{0:T(1024)S(1)} %iota.30, s32[]{:T(128)} %constant.109.clone.1), kind=kCustom, calls=%fused_computation.65 | custom fusion | bytes 4100 | tf_op jit(solution)/shard_map/scatter | solution.py:33
  12.4 3.9 %copy.28 = bf16[1,1024,1024]{1,2,0:T(8,128)(2,1)} copy(bf16[1,1024,1024]{2,1,0:T(8,128)(2,1)} %param.10) | data formatting | bytes 4194304 | tf_op args[2]
  16.3 0.0 copy-start.5
  16.4 8.0 %gather_fusion = bf16[1024,1024]{1,0:T(8,128)(2,1)} fusion(bf16[1024,1024]{0,1:T(8,128)(2,1)} %bitcast.57, s32[1024]{0:T(1024)S(1)} %fusion.22), kind=kCustom, calls=%fused_computation | custom fusion | bytes 4198400 | tf_op jit(solution)/shard_map/jit(_take)/gather | solution.py:34
  24.3 0.0 copy-done.5
  24.3 0.0 copy-start.3
  24.3 0.0 copy-start.4
  24.3 3.8 fusion.9
  28.1 0.0 all-gather.2.cloned.1.call-update
  28.1 0.0 copy-done.3
  28.2 0.0 copy-done.4
  28.2 0.1 compare_bitcast_fusion
  28.2 0.1 fusion.16
  28.3 0.1 select_reduce_fusion.2
  28.5 0.1 broadcast_bitcast_fusion.1
  28.5 0.1 broadcast_bitcast_fusion
  28.6 0.0 copy-done
  28.6 2.5 select_convert_fusion
  31.1 0.0 copy-start.6
  31.1 100.1 %all-gather.2.cloned.1.call-done = bf16[1024,7168]{0,1:T(8,128)(2,1)} async-done(((bf16[1024,448]{0,1:T(8,128)(2,1)}), bf16[1024,7168]{0,1:T(8,128)(2,1)}) %all-gather.2.cloned.1.call-update) | async-done | bytes 14680080 | tf_op jit(solution)/shard_map/all_gather | solution.py:50
  131.2 22.5 %fusion.1 = bf16[64,56,8,128]{3,2,1,0:T(8,128)(2,1)} fusion(bf16[512,1024]{1,0:T(8,128)(2,1)S(1)} %select_convert_fusion, bf16[1024,7168]{0,1:T(8,128)(2,1)} %all-gather.2.cloned.1.call-done, bf16[512,8192]{1,0:T(8,128)(2,1)} %bitcast.69), kind=kOutput, calls=%fused_computation.12 | convolution fusion | flops 7527202816 | bytes 30408704 | tf_op jit(solution)/shard_map/dot_general | solution.py:48
  153.7 0.0 copy-done.6
  153.7 8.2 %copy.39 = bf16[64,56,8,128]{3,2,0,1:T(8,128)(2,1)} copy(bf16[64,56,8,128]{3,2,1,0:T(8,128)(2,1)} %fusion.1) | data formatting | bytes 14680064 | tf_op jit(solution)/shard_map/reshape | solution.py:61
  161.9 8.6 %gather_fusion.1 = bf16[64,512,128]{2,1,0:T(8,128)(2,1)} fusion(bf16[512,56,128]{2,0,1:T(8,128)(2,1)} %bitcast.60, s32[1024]{0:T(1024)S(1)} %pad_clamp_fusion.1), kind=kCustom, calls=%fused_computation.1 | custom fusion | bytes 16777472 | tf_op jit(solution)/shard_map/jit(_take)/gather | solution.py:62
  170.5 12.0 %copy.30 = bf16[512,64,128]{2,1,0:T(8,128)(2,1)} copy(bf16[512,64,128]{2,0,1:T(8,128)(2,1)} %bitcast.61) | data formatting | bytes 16777216 | tf_op jit(solution)/shard_map/jit(_take)/gather | solution.py:62
  182.5 13.3 %gather.28 = bf16[4,128,8192]{2,1,0:T(8,128)(2,1)} reshape(bf16[512,64,128]{2,1,0:T(8,128)(2,1)} %copy.30) | data formatting | bytes 16777216 | tf_op jit(solution)/shard_map/jit(_take)/gather | solution.py:62
  195.8 7.3 %broadcast_select_fusion = bf16[4,128,8192]{2,1,0:T(8,128)(2,1)} fusion(bf16[4,128,8192]{2,1,0:T(8,128)(2,1)} %gather.28, pred[8192]{0:T(1024)(128)(4,1)S(1)} %broadcast_bitcast_fusion), kind=kLoop, calls=%fused_computation.9 | loop fusion | flops 4194304 | bytes 16785408 | tf_op jit(solution)/shard_map/jit(_take)/select_n | solution.py:62
  203.0 13.6 %copy.31 = bf16[4,128,8192]{1,0,2:T(4,128)(2,1)} copy(bf16[4,128,8192]{2,1,0:T(8,128)(2,1)} %broadcast_select_fusion) | data formatting | bytes 16777216 | tf_op jit(solution)/shard_map/jit(_take)/select_n | solution.py:62
  216.7 8.6 %all-to-all-start = ((bf16[4,128,8192]{1,0,2:T(4,128)(2,1)}), bf16[4,128,8192]{1,0,2:T(4,128)(2,1)}, u32[]{:S(2)}, u32[]{:S(2)}) async-start(bf16[4,128,8192]{1,0,2:T(4,128)(2,1)} %copy.31), calls=%async_computation | async-start | bytes 16777216 | tf_op jit(solution)/shard_map/all_to_all | solution.py:78
  225.2 0.1 fusion.15
  225.4 0.1 reduce_or.25
  225.5 0.1 select_reduce_fusion.1
  225.6 0.1 reduce_sum.38
  225.7 0.1 reshape.308
  225.8 0.1 add.214
  225.9 0.2 select_reduce_fusion
  226.1 2.6 gather_fusion.3
  228.7 0.1 gather.26
  228.9 96.0 %all-to-all-done = bf16[4,128,8192]{1,0,2:T(4,128)(2,1)} async-done(((bf16[4,128,8192]{1,0,2:T(4,128)(2,1)}), bf16[4,128,8192]{1,0,2:T(4,128)(2,1)}, u32[]{:S(2)}, u32[]{:S(2)}) %all-to-all-start) | async-done | bytes 8388640 | tf_op jit(solution)/shard_map/all_to_all | solution.py:78
  325.0 7.7 %copy.32 = bf16[4,128,8192]{1,2,0:T(8,128)(2,1)} copy(bf16[4,128,8192]{1,0,2:T(4,128)(2,1)} %all-to-all-done) | data formatting | bytes 16777216 | tf_op jit(solution)/shard_map/all_to_all | solution.py:78
  332.6 9.6 %copy.33 = bf16[128,4,128,64]{2,3,1,0:T(8,128)(2,1)} copy(bf16[128,4,128,64]{2,3,0,1:T(8,128)(2,1)} %bitcast.62) | data formatting | bytes 16777216 | tf_op jit(solution)/shard_map/all_to_all | solution.py:78
  342.3 23.0 %gather_fusion.2 = bf16[512,128,64]{1,2,0:T(8,128)(2,1)} fusion(bf16[512,128,64]{1,2,0:T(8,128)(2,1)} %bitcast.59, s32[1024]{0:T(1024)S(1)} %pad_clamp_fusion), kind=kCustom, calls=%fused_computation.2 | custom fusion | bytes 16779264 | tf_op jit(solution)/shard_map/jit(_take)/gather | solution.py:82
  365.2 0.0 copy-start.2
  365.2 0.0 copy-start.1
  365.2 5.6 %broadcast_select_fusion.1 = bf16[4,2,64,128,64]{3,4,2,1,0:T(8,128)(2,1)S(1)} fusion(bf16[4,2,64,128,64]{3,4,2,1,0:T(8,128)(2,1)} %bitcast.58, pred[4,2,64]{2,1,0:T(4,128)(4,1)S(1)} %compare_and_fusion), kind=kLoop, calls=%fused_computation.10 | loop fusion | flops 4194304 | bytes 16777728 | tf_op jit(solution)/shard_map/jit(_take)/select_n | solution.py:82
  370.8 0.0 copy-done.2
  370.8 3.0 fusion
  373.8 0.0 copy-done.1
  (13 shorter events, 0.2 us)
Async XLA Ops:
  7.2 21.5 %copy-start = (bf16[1,1024,1024]{2,1,0:T(8,128)(2,1)S(1)}, bf16[1,1024,1024]{2,1,0:T(8,128)(2,1)}, u32[]{:S(2)}) copy-start(bf16[1,1024,1024]{2,1,0:T(8,128)(2,1)} %param.11) | copy-start | bytes 6291460
  7.2 124.0 %all-gather.2.cloned.1.call-start = ((), (), s32[]{:S(2)}) async-start(), calls=%async_computation.1 | async-start | bytes 15597568 | tf_op jit(solution)/shard_map/all_gather | solution.py:50
  16.3 8.0 %copy-start.5 = (bf16[1,1024,448]{1,2,0:T(8,128)(2,1)S(1)}, bf16[1,1024,448]{1,2,0:T(8,128)(2,1)}, u32[]{:S(2)}) copy-start(bf16[1,1024,448]{1,2,0:T(8,128)(2,1)} %param.8) | copy-start | bytes 2752516
  24.3 3.8 copy-start.3
  24.3 3.8 %copy-start.4 = (s32[8,64]{1,0:T(8,128)S(1)}, s32[8,64]{1,0:T(8,128)}, u32[]{:S(2)}) copy-start(s32[8,64]{1,0:T(8,128)} %param.13) | copy-start | bytes 6148
  31.1 122.6 %copy-start.6 = (bf16[512,1024]{1,0:T(8,128)(2,1)}, bf16[512,1024]{1,0:T(8,128)(2,1)S(1)}, u32[]{:S(2)}) copy-start(bf16[512,1024]{1,0:T(8,128)(2,1)S(1)} %select_convert_fusion) | copy-start | bytes 3145732
  216.7 108.3 %all-to-all-start = ((bf16[4,128,8192]{1,0,2:T(4,128)(2,1)}), bf16[4,128,8192]{1,0,2:T(4,128)(2,1)}, u32[]{:S(2)}, u32[]{:S(2)}) async-start(bf16[4,128,8192]{1,0,2:T(4,128)(2,1)} %copy.31), calls=%async_computation | async-start | bytes 16777216 | tf_op jit(solution)/shard_map/all_to_all | solution.py:78
  365.2 5.6 %copy-start.2 = (bf16[4,64,8192]{2,1,0:T(8,128)(2,1)S(1)}, bf16[4,64,8192]{2,1,0:T(8,128)(2,1)}, u32[]{:S(2)}) copy-start(bf16[4,64,8192]{2,1,0:T(8,128)(2,1)} %param.15) | copy-start | bytes 12582916
  365.2 8.6 %copy-start.1 = (bf16[1,1024,1024]{2,1,0:T(8,128)(2,1)S(1)}, bf16[1,1024,1024]{2,1,0:T(8,128)(2,1)}, u32[]{:S(2)}) copy-start(bf16[1,1024,1024]{2,1,0:T(8,128)(2,1)} %param.11) | copy-start | bytes 6291460
Sparse Core Ops, SparseCore 0:
  28.2 102.9 all-gather.1
where the time goes:
time: 382 us; the launch traced here: 381 us
  waiting for transfers between devices  196 us (51%)
  local copies, waits for them, and re-layouts  115 us (30%)
  matrix products  28.7 us (8%)
  other arithmetic  17.5 us (5%)
  between operations  14.2 us (4%)
  starting transfers between devices  8.6 us (2%)
    all_gather x1, waiting for transfers between devices, shards(): lax.all_gather(upper_part, 'row', axis=1, tiled=True)  100 us
    all_to_all x1, waiting for transfers between devices, shards(): lax.all_to_all(spread, ('row', 'col'), split_axis=2, concat_axis=0, tiled...  96 us
    gather x3, local copies, waits for them, and re-layouts, shards(): spread = jnp.take(blocked, source_block, axis=1, mode='fill', fill_value=0)  33.9 us
    gather x1, local copies, waits for them, and re-layouts, shards(): jnp.take(arrived, item_index.reshape(-1), axis=0, mode='fill', fill_value=0)  23 us
    dot_general x1, matrix products, shards(): jnp.dot(lower_factor, lax.all_gather(upper_part, 'row', axis=1, tiled=Tru...  22.5 us
    all_to_all x2, local copies, waits for them, and re-layouts, shards(): lax.all_to_all(spread, ('row', 'col'), split_axis=2, concat_axis=0, tiled...  17.3 us
    select_n x1, local copies, waits for them, and re-layouts, shards(): spread = jnp.take(blocked, source_block, axis=1, mode='fill', fill_value=0)  13.6 us
    all_to_all x1, starting transfers between devices, shards(): lax.all_to_all(spread, ('row', 'col'), split_axis=2, concat_axis=0, tiled...  8.56 us
  transfers between devices with their start and end apart: 2, of which 2 were waited for; matrix products, arithmetic and copies ran while one was open for 2% of the time, Pallas kernels for 0%

commit v1 on v0

v1 whole, which is shorter than its diff:
```python
import jax
import jax.numpy as jnp
from jax import lax
from jax.experimental import pallas as pl
from jax.experimental.pallas import tpu as pltpu
from jax.sharding import PartitionSpec as P

MIB = 1024 * 1024
NT = (((1,), (1,)), ((), ()))


def factor_kernel(
    slot_block,
    order,
    rows,
    inverse_lower,
    inverse_upper,
    front,
    upper_out,
    lower_out,
):
    row_index = lax.axis_index("row")
    col_index = lax.axis_index("col")
    slot_count, block_rows, pivots = lower_out.shape[1:]
    target = lax.broadcasted_iota(jnp.int32, (pivots, pivots), 0)
    chosen = jnp.where(target == order[...], 1.0, 0.0).astype(jnp.bfloat16)
    permuted = jnp.dot(rows[0], chosen, preferred_element_type=jnp.float32).astype(jnp.bfloat16)
    upper = lax.dot_general(permuted, inverse_lower[0], NT, preferred_element_type=jnp.float32)
    upper_out[...] = upper.astype(jnp.bfloat16)
    for s in range(slot_count):
        live = slot_block[col_index, row_index * slot_count + s] >= 0
        lower = jnp.dot(front[0, s], inverse_upper[0], preferred_element_type=jnp.float32)
        lower_out[0, s] = jnp.where(live, lower, 0.0).astype(jnp.bfloat16)


def factor(slot_block, order, rows, inverse_lower, inverse_upper, front):
    pivots = inverse_lower.shape[1]
    width = rows.shape[1]
    slots, block_rows = front.shape[1:3]
    whole = lambda shape: pl.BlockSpec(shape, lambda i: (0,) * len(shape))
    return pl.pallas_call(
        factor_kernel,
        grid=(1,),
        out_shape=(
            jax.ShapeDtypeStruct((width, pivots), jnp.bfloat16),
            jax.ShapeDtypeStruct((1, slots, block_rows, pivots), jnp.bfloat16),
        ),
        in_specs=[
            pl.BlockSpec(memory_space=pltpu.SMEM),
            whole(order.shape),
            whole(rows.shape),
            whole(inverse_lower.shape),
            whole(inverse_upper.shape),
            whole((1, slots, block_rows, pivots)),
        ],
        out_specs=(
            whole((width, pivots)),
            whole((1, slots, block_rows, pivots)),
        ),
        compiler_params=pltpu.CompilerParams(vmem_limit_bytes=48 * MIB),
    )(slot_block, order, rows, inverse_lower, inverse_upper, front)


def schur_kernel(parent_map, upper_t, lower, front, spread):
    step = pl.program_id(0)
    col_index = lax.axis_index("col")
    slots, block_rows, pivots = lower.shape[1:]
    blocks = upper_t.shape[0] // block_rows
    lower_flat = lower[0].reshape(slots * block_rows, pivots)

    @pl.when(step == 0)
    def _():
        spread[...] = jnp.zeros_like(spread)

    for b in range(blocks):
        product = lax.dot_general(
            upper_t[pl.ds(b * block_rows, block_rows)],
            lower_flat,
            NT,
            preferred_element_type=jnp.float32,
        )
        target = parent_map[col_index, step * blocks + b]
        for s in range(slots):
            lanes = pl.ds(s * block_rows, block_rows)
            own = front[0, s, :, pl.ds(b * block_rows, block_rows)].astype(jnp.float32).T
            value = own - product[:, s * block_rows : (s + 1) * block_rows]
            spread[pl.ds(target * 2, 2), :, lanes] = value.astype(jnp.bfloat16).reshape(
                2, block_rows // 2, block_rows
            )


def schur(parent_map, upper_t, lower, front, devices):
    slots, block_rows, pivots = lower.shape[1:]
    trailing = upper_t.shape[0]
    steps = 8
    width = trailing // steps
    return pl.pallas_call(
        schur_kernel,
        grid=(steps,),
        out_shape=jax.ShapeDtypeStruct((devices, 64, slots * block_rows), jnp.bfloat16),
        in_specs=[
            pl.BlockSpec(memory_space=pltpu.SMEM),
            pl.BlockSpec((width, pivots), lambda i: (i, 0)),
            pl.BlockSpec((1, slots, block_rows, pivots), lambda i: (0, 0, 0, 0)),
            pl.BlockSpec(
                (pl.Element(1), pl.Element(slots), pl.Element(block_rows), pl.Element(width)),
                lambda i: (0, 0, 0, pl.multiple_of(pivots + i * width, 128)),
            ),
        ],
        out_specs=pl.BlockSpec((devices, 64, slots * block_rows), lambda i: (0, 0, 0)),
        compiler_params=pltpu.CompilerParams(vmem_limit_bytes=48 * MIB),
    )(parent_map, upper_t, lower, front)


def assemble_kernel(place, arrived, initial, out):
    parent = pl.program_id(0)
    block_rows = 128
    slots = arrived.shape[3] // block_rows

    def one(block, carry):
        lanes = pl.ds(pl.multiple_of(block * block_rows, block_rows), block_rows)
        total = None
        for child in range(2):
            at = place[parent * 2 + child, block]
            safe = jnp.maximum(at, 0)
            slot_lanes = pl.ds(
                pl.multiple_of(lax.rem(safe, slots) * block_rows, block_rows), block_rows
            )
            value = arrived[lax.div(safe, slots), child, :, slot_lanes].astype(jnp.float32)
            value = jnp.where(at >= 0, value, 0.0)
            total = value if total is None else total + value
        out[0, :, lanes] = (initial[0, :, lanes].astype(jnp.float32) + total).astype(jnp.bfloat16)
        return carry

    lax.fori_loop(0, out.shape[2] // block_rows, one, 0, unroll=4)


def assemble(place, arrived, initial):
    parents, piece, order = initial.shape
    rows, fronts, _, width = arrived.shape
    return pl.pallas_call(
        assemble_kernel,
        grid=(parents,),
        out_shape=jax.ShapeDtypeStruct(initial.shape, initial.dtype),
        in_specs=[
            pl.BlockSpec(memory_space=pltpu.SMEM),
            pl.BlockSpec((rows, 2, piece, width), lambda p: (0, p, 0, 0)),
            pl.BlockSpec((1, piece, order), lambda p: (p, 0, 0)),
        ],
        out_specs=pl.BlockSpec((1, piece, order), lambda p: (p, 0, 0)),
        compiler_params=pltpu.CompilerParams(vmem_limit_bytes=48 * MIB),
    )(place, arrived, initial)


def places(slot_block, parent_map, parent_blocks):
    block_ids = jnp.arange(parent_map.shape[1], dtype=jnp.int32)
    hit = slot_block[:, :, None] == block_ids[None, None, :]
    target = jnp.sum(jnp.where(hit, parent_map[:, None, :] + 1, 0), axis=2) - 1
    parent_ids = jnp.arange(parent_blocks, dtype=jnp.int32)
    slot_ids = jnp.arange(slot_block.shape[1], dtype=jnp.int32)
    match = target[:, None, :] == parent_ids[None, :, None]
    return jnp.sum(jnp.where(match, slot_ids[None, None, :] + 1, 0), axis=2) - 1


def shards(
    pivot_rows,
    pivot_order,
    inverse_lower,
    inverse_upper,
    front_rows,
    slot_block,
    parent_map,
    parent_init,
):
    rows, cols = lax.axis_size("row"), lax.axis_size("col")
    columns = jnp.swapaxes(pivot_rows, 1, 2)
    upper_t, lower = factor(
        slot_block, pivot_order, columns, inverse_lower, inverse_upper, front_rows
    )
    gathered = lax.all_gather(upper_t, "row", axis=0, tiled=True)
    spread = schur(parent_map, gathered, lower, front_rows, rows * cols)
    arrived = lax.all_to_all(spread, ("row", "col"), split_axis=0, concat_axis=0, tiled=True)
    place = places(slot_block, parent_map, parent_init.shape[2] // front_rows.shape[2])
    assembled = assemble(place, arrived.reshape(rows, cols, *arrived.shape[1:]), parent_init)
    return (lower, upper_t.T[None], assembled)


def solution(mesh):
    return jax.shard_map(
        shards,
        mesh=mesh,
        in_specs=(
            P("col", None, "row"),
            P("col", None),
            P("col", None, None),
            P("col", None, None),
            P("col", "row", None, None),
            P(),
            P(),
            P(None, ("row", "col"), None),
        ),
        out_specs=(
            P("col", "row", None, None),
            P("col", None, "row"),
            P(None, ("row", "col"), None),
        ),
        check_vma=False,
    )
```

time: 382 us -> 274 us (0.72)
  local copies, waits for them, and re-layouts: 115 us -> 9.15 us
  Pallas kernels: 0 us -> 39.3 us
  matrix products: 28.7 us -> 0 us
  other arithmetic: 17.5 us -> 0.36 us
  waiting for transfers between devices: 196 us -> 202 us
    gather x8 -> x0, local copies, waits for them, and re-layouts: 67.6 us -> none  [the longest x3 33.9 us: shards(): spread = jnp.take(blocked, source_block, axis=1, mode='fill', fill_value=0)]
    pallas_call x0 -> x3, Pallas kernels: none -> 39.3 us  [the longest x1 26.1 us: schur(): pl.pallas_call(schur_kernel, grid=(steps,), out_shape=jax.ShapeDtypeStruc...]
    dot_general x3 -> x0, matrix products: 28.7 us -> none  [the longest x1 22.5 us: shards(): jnp.dot(lower_factor, lax.all_gather(upper_part, 'row', axis=1, tiled=Tru...]
    all_to_all x2 -> x0, local copies, waits for them, and re-layouts: 17.3 us -> none  [shards(): lax.all_to_all(spread, ('row', 'col'), split_axis=2, concat_axis=0, tiled...]
    select_n x5 -> x0, other arithmetic: 13.7 us -> none  [the longest x2 7.27 us: shards(): spread = jnp.take(blocked, source_block, axis=1, mode='fill', fill_value=0)]
    select_n x1 -> x0, local copies, waits for them, and re-layouts: 13.6 us -> none  [shards(): spread = jnp.take(blocked, source_block, axis=1, mode='fill', fill_value=0)]
    reshape x1 -> x0, local copies, waits for them, and re-layouts: 8.16 us -> none  [shards(): schur_rows.reshape(slot_count * block_rows, block_count, block_rows)]
    unnamed x15 -> x18, local copies, waits for them, and re-layouts: 3.98 us -> 9.15 us
  transfers between devices with their start and end apart: 2 -> 2, of which waited for: 2 -> 2; matrix products, arithmetic and copies ran while one was open for 2% -> 0% of each run, Pallas kernels for 0% -> 0%
where the time goes in v1:
time: 274 us
  waiting for transfers between devices  202 us (74%)
  Pallas kernels  39.3 us (14%)
  between operations  14.1 us (5%)
  local copies, waits for them, and re-layouts  9.15 us (3%)
  starting transfers between devices  8.56 us (3%)
    all_gather x1, waiting for transfers between devices, shards(): gathered = lax.all_gather(upper_t, 'row', axis=0, tiled=True)  103 us
    all_to_all x1, waiting for transfers between devices, shards(): lax.all_to_all(spread, ('row', 'col'), split_axis=0, concat_axis=0, tiled...  99.3 us
    pallas_call x1, Pallas kernels, schur(): pl.pallas_call(schur_kernel, grid=(steps,), out_shape=jax.ShapeDtypeStruc...  26.1 us
    unnamed x18, local copies, waits for them, and re-layouts  9.15 us
    all_to_all x1, starting transfers between devices, shards(): lax.all_to_all(spread, ('row', 'col'), split_axis=0, concat_axis=0, tiled...  8.52 us
    pallas_call x1, Pallas kernels, assemble(): pl.pallas_call(assemble_kernel, grid=(parents,), out_shape=jax.ShapeDtype...  7.64 us
    pallas_call x1, Pallas kernels, factor(): pl.pallas_call(factor_kernel, grid=(1,), out_shape=(jax.ShapeDtypeStruct(...  5.58 us
  transfers between devices with their start and end apart: 2, of which 2 were waited for; matrix products, arithmetic and copies ran while one was open for 0% of the time, Pallas kernels for 0%

profile of v1, /device:TPU:15, one launch (start us, length us, event | category | flops | bytes accessed | tf_op | source)
XLA Modules:
  0.0 273.9 jit_solution(8543481983236683817)
XLA Ops:
  7.2 0.0 all-gather.2.cloned.1.call-start
  7.2 0.0 copy-start.1
  7.2 1.6 copy-done.1
  8.8 0.0 copy-start.2
  8.8 1.6 copy-done.2
  10.4 0.0 copy-start.4
  10.4 1.2 copy-done.4
  11.6 0.0 copy-start.5
  11.6 0.7 copy-done.5
  12.3 0.0 copy-start.8
  12.3 0.7 copy-done.8
  12.9 0.0 copy-start.7
  13.0 5.6 %shard_map.103 = (bf16[448,1024]{1,0:T(8,128)(2,1)}, bf16[1,4,128,1024]{3,2,1,0:T(8,128)(2,1)}) custom-call(s32[8,64]{1,0:T(8,128)S(1)} %copy-done.5, s32[1,1024]{1,0:T(1,128)S(1)} %copy-done.8, bf16[1,448,1024]{2,1,0:T(8,128)(2,1)S(1)} %bitcast.5, bf16[1,1024,1024]{2,1,0:T(8,128)(2,1)S(1)} %copy-done.1, bf16[1,1024,1024]{2,1,0:T(8,128)(2,1)S(1)} %copy-done.2, ...), custom_call_target="tpu_custom_call" | custom-call | tf_op jit(solution)/shard_map/pallas_call | solution.py:41
  18.5 0.0 all-gather.2.cloned.1.call-update
  18.6 103.1 %all-gather.2.cloned.1.call-done.upper_t = bf16[7168,1024]{1,0:T(8,128)(2,1)} async-done(((bf16[448,1024]{1,0:T(8,128)(2,1)}), bf16[7168,1024]{1,0:T(8,128)(2,1)}) %all-gather.2.cloned.1.call-update) | async-done | bytes 14680080 | tf_op jit(solution)/shard_map/all_gather | solution.py:180
  121.6 0.0 copy-done.7
  121.6 0.0 copy-start.3
  121.6 1.2 copy-done.3
  122.9 26.1 %shard_map.104 = bf16[128,64,512]{2,1,0:T(8,128)(2,1)} custom-call(s32[8,56]{1,0:T(8,128)S(1)} %copy-done.7, bf16[7168,1024]{1,0:T(8,128)(2,1)} %all-gather.2.cloned.1.call-done.upper_t, bf16[1,4,128,1024]{3,2,1,0:T(8,128)(2,1)S(1)} %copy-done.3, bf16[1,4,128,8192]{3,2,1,0:T(8,128)(2,1)} %front.3), custom_call_target="tpu_custom_call" | custom-call | tf_op jit(solution)/shard_map/pallas_call | solution.py:97
  148.9 0.0 copy-start.6
  148.9 8.5 %all-to-all-start = ((bf16[128,64,512]{2,1,0:T(8,128)(2,1)}), bf16[128,64,512]{2,1,0:T(8,128)(2,1)}, u32[]{:S(2)}, u32[]{:S(2)}) async-start(bf16[128,64,512]{2,1,0:T(8,128)(2,1)} %shard_map.104), calls=%async_computation | async-start | bytes 16777216 | tf_op jit(solution)/shard_map/all_to_all | solution.py:182
  157.5 0.0 copy-done.6
  157.5 0.1 select_reduce_fusion.1
  157.7 0.2 select_reduce_fusion
  157.9 99.3 %all-to-all-done = bf16[128,64,512]{2,1,0:T(8,128)(2,1)} async-done(((bf16[128,64,512]{2,1,0:T(8,128)(2,1)}), bf16[128,64,512]{2,1,0:T(8,128)(2,1)}, u32[]{:S(2)}, u32[]{:S(2)}) %all-to-all-start) | async-done | bytes 8388640 | tf_op jit(solution)/shard_map/all_to_all | solution.py:182
  257.2 0.0 copy-start
  257.2 2.2 copy-done
  259.4 7.6 %shard_map.105 = bf16[4,64,8192]{2,1,0:T(8,128)(2,1)} custom-call(s32[8,64]{1,0:T(8,128)S(1)} %broadcast_add_fusion.place, bf16[16,8,64,512]{3,2,1,0:T(8,128)(2,1)} %bitcast.3.arrived, bf16[4,64,8192]{2,1,0:T(8,128)(2,1)S(1)} %copy-done), custom_call_target="tpu_custom_call" | custom-call | tf_op jit(solution)/shard_map/pallas_call | solution.py:141
  (4 shorter events, 0.0 us)
Async XLA Ops:
  7.2 114.5 %all-gather.2.cloned.1.call-start = ((), (), s32[]{:S(2)}) async-start(), calls=%async_computation.1 | async-start | bytes 15597568 | tf_op jit(solution)/shard_map/all_gather | solution.py:180
  7.2 1.6 copy-start.1
  8.8 1.6 copy-start.2
  10.4 1.2 copy-start.4
  11.6 0.7 copy-start.5
  12.3 0.7 copy-start.8
  12.9 108.7 %copy-start.7 = (s32[8,56]{1,0:T(8,128)S(1)}, s32[8,56]{1,0:T(8,128)}, u32[]{:S(2)}) copy-start(s32[8,56]{1,0:T(8,128)} %parent_map.1) | copy-start | bytes 5380
  121.6 1.2 copy-start.3
  148.9 8.6 %copy-start.6 = (s32[8,64]{1,0:T(8,128)S(1)}, s32[8,64]{1,0:T(8,128)}, u32[]{:S(2)}) copy-start(s32[8,64]{1,0:T(8,128)} %slot_block.1) | copy-start | bytes 6148
  148.9 108.2 %all-to-all-start = ((bf16[128,64,512]{2,1,0:T(8,128)(2,1)}), bf16[128,64,512]{2,1,0:T(8,128)(2,1)}, u32[]{:S(2)}, u32[]{:S(2)}) async-start(bf16[128,64,512]{2,1,0:T(8,128)(2,1)} %shard_map.104), calls=%async_computation | async-start | bytes 16777216 | tf_op jit(solution)/shard_map/all_to_all | solution.py:182
  257.2 2.2 copy-start
Sparse Core Ops, SparseCore 0:
  18.7 102.9 all-gather.1

commit v2 on v1

v2 whole, which is shorter than its diff:
```python
import jax
import jax.numpy as jnp
from jax import lax
from jax.experimental import pallas as pl
from jax.experimental.pallas import tpu as pltpu
from jax.sharding import PartitionSpec as P

MIB = 1024 * 1024
NT = (((1,), (1,)), ((), ()))


def factor_and_update(
    source_block,
    slot_block,
    order,
    rows,
    inverse_lower,
    inverse_upper,
    front,
    upper_out,
    lower_out,
    spread_out,
    gathered,
    child,
    spread,
    chosen,
    rows_held,
    inverse_lower_held,
    inverse_upper_held,
    lead,
    lower,
    trailing,
    send_sem,
    recv_sem,
    load_sem,
    trailing_sem,
    store_sem,
    spread_sem,
):
    row_index = lax.axis_index("row")
    col_index = lax.axis_index("col")
    z, x = row_index // 4, lax.rem(row_index, 4)
    slots, block_rows, pivots = lead.shape
    width = rows_held.shape[0]
    quarter = width // 4
    pair_width = 2 * width
    pair_blocks = pair_width // block_rows

    def at_row(dz, dx):
        return lax.rem(z + dz + 4, 4) * 4 + lax.rem(x + dx + 4, 4)

    def load(source, target, sem):
        copy = pltpu.make_async_copy(source, target, sem)
        copy.start()
        return copy

    rows_in = load(rows.at[0], rows_held, load_sem.at[0])
    inverse_lower_in = load(inverse_lower.at[0], inverse_lower_held, load_sem.at[1])
    lead_in = load(front.at[0, :, :, pl.ds(0, pivots)], lead, load_sem.at[2])
    inverse_upper_in = load(inverse_upper.at[0], inverse_upper_held, load_sem.at[3])

    barrier = pltpu.get_barrier_semaphore()
    for dz, dx in ((0, 1), (0, -1), (1, 0), (-1, 0)):
        pl.semaphore_signal(
            barrier,
            inc=1,
            device_id=(at_row(dz, dx), col_index),
            device_id_type=pl.DeviceIdType.MESH,
        )

    target = lax.broadcasted_iota(jnp.int32, (pivots, pivots), 0)
    chosen[...] = jnp.where(target == order[...], 1.0, 0.0).astype(jnp.bfloat16)
    rows_in.wait()
    inverse_lower_in.wait()

    def place(offset, part):
        start = at_row(*offset) * width + part * quarter
        return gathered.at[pl.ds(pl.multiple_of(start, 16), quarter)]

    numbers = {}
    sent = []

    def message(offset, part, axis, step):
        number = numbers.setdefault((offset, part, axis, step), len(numbers))
        toward = (step, 0) if axis == 0 else (0, step)
        return pltpu.make_async_remote_copy(
            src_ref=place(offset, part),
            dst_ref=place(offset, part),
            send_sem=send_sem.at[number],
            recv_sem=recv_sem.at[number],
            device_id=(at_row(*toward), col_index),
            device_id_type=pl.DeviceIdType.MESH,
        )

    def receiver_offset(offset, axis, step):
        moved = list(offset)
        moved[axis] -= step
        if moved[axis] == -2:
            moved[axis] = 2
        return tuple(moved)

    def send(offset, part, axis, step):
        key = (receiver_offset(offset, axis, step), part, axis, step)
        number = numbers.setdefault(key, len(numbers))
        toward = (step, 0) if axis == 0 else (0, step)
        copy = pltpu.make_async_remote_copy(
            src_ref=place(offset, part),
            dst_ref=place(offset, part),
            send_sem=send_sem.at[number],
            recv_sem=recv_sem.at[number],
            device_id=(at_row(*toward), col_index),
            device_id_type=pl.DeviceIdType.MESH,
        )
        copy.start()
        sent.append(copy)

    def receive(offset, part, axis, step):
        message(offset, part, axis, step).wait_recv()

    parts = ((0, 1), (2, 3))
    first = (1, 0)
    second = (0, 1)

    def offset_of(half, near, far):
        return (far, near) if half == 0 else (near, far)

    for part in (0, 2, 1, 3):
        span = pl.ds(part * quarter, quarter)
        permuted = jnp.dot(rows_held[span], chosen[...], preferred_element_type=jnp.float32)
        upper = lax.dot_general(
            permuted.astype(jnp.bfloat16),
            inverse_lower_held[...],
            NT,
            preferred_element_type=jnp.float32,
        )
        start = pl.multiple_of(row_index * width + part * quarter, 16)
        gathered[pl.ds(start, quarter)] = upper.astype(jnp.bfloat16)
        if part == 0:
            pl.semaphore_wait(barrier, 4)
        half = part // 2
        for step in (1, -1):
            send((0, 0), part, first[half], step)
        for step in (1, -1):
            send((0, 0), part, second[half], step)
    own = pl.ds(pl.multiple_of(row_index * width, 16), width)
    upper_done = load(gathered.at[own], upper_out, store_sem.at[0])

    def trailing_of(pair, buffer):
        start = pl.multiple_of(pivots + pair * pair_width, 128)
        return pltpu.make_async_copy(
            front.at[0, :, :, pl.ds(start, pair_width)],
            trailing.at[buffer],
            trailing_sem.at[buffer],
        )

    def pair_at(dz, far):
        half = x // 2
        return lax.rem(z + dz + 4, 4) * 2 + (1 - half if far else half)

    pairs = [
        pair_at(0, 0),
        pair_at(-1, 0),
        pair_at(1, 0),
        pair_at(0, 1),
        pair_at(2, 0),
        pair_at(-1, 1),
        pair_at(1, 1),
        pair_at(2, 1),
    ]
    trailing_of(pairs[0], 0).start()
    trailing_of(pairs[1], 1).start()

    lead_in.wait()
    inverse_upper_in.wait()
    for s in range(slots):
        live = slot_block[col_index, row_index * slots + s] >= 0
        value = jnp.dot(lead[s], inverse_upper_held[...], preferred_element_type=jnp.float32)
        lower[pl.ds(s * block_rows, block_rows)] = jnp.where(live, value, 0.0).astype(jnp.bfloat16)
    lower_done = load(lower, lower_out, store_sem.at[1])

    def update(turn):
        pair, buffer = pairs[turn], turn % 2
        trailing_of(pair, buffer).wait()

        def one(b, carry):
            start = pl.multiple_of(pair * pair_width + b * block_rows, block_rows)
            product = lax.dot_general(
                gathered[pl.ds(start, block_rows)],
                lower[...],
                NT,
                preferred_element_type=jnp.float32,
            )
            columns = pl.ds(pl.multiple_of(b * block_rows, block_rows), block_rows)
            for s in range(slots):
                held = trailing[buffer, s, :, columns].astype(jnp.float32).T
                value = held - product[:, s * block_rows : (s + 1) * block_rows]
                child[
                    pl.ds((pair * pair_blocks + b) * 2, 2), :, pl.ds(s * block_rows, block_rows)
                ] = value.astype(jnp.bfloat16).reshape(2, block_rows // 2, block_rows)
            return carry

        lax.fori_loop(0, pair_blocks, one, 0)
        if turn + 2 < len(pairs):
            trailing_of(pairs[turn + 2], buffer).start()

    def each():
        for k in range(2):
            for half in range(2):
                for step in (1, -1):
                    yield k, half, step, parts[half][k]

    def relay(near):
        for k, half, step, part in each():
            offset = offset_of(half, near, -step)
            receive(offset, part, second[half], step)
            if (k == 0) == (step == 1):
                send(offset, part, second[half], step)

    def finish(near):
        for k in range(2):
            for half in range(2):
                step = 1 if k == 0 else -1
                receive(offset_of(half, near, 2), parts[half][k], second[half], step)

    for k, half, step, part in each():
        offset = offset_of(half, -step, 0)
        receive(offset, part, first[half], step)
        if (k == 0) == (step == 1):
            send(offset, part, first[half], step)
        for other in (1, -1):
            send(offset, part, second[half], other)
    relay(0)
    for k in range(2):
        for half in range(2):
            step = 1 if k == 0 else -1
            offset = offset_of(half, 2, 0)
            receive(offset, parts[half][k], first[half], step)
            for other in (1, -1):
                send(offset, parts[half][k], second[half], other)
    update(0)
    relay(-1)
    relay(1)
    update(1)
    update(2)
    finish(0)
    relay(2)
    update(3)
    finish(-1)
    finish(1)
    update(4)
    update(5)
    update(6)
    finish(2)
    update(7)

    groups = spread_sem.shape[0]
    parent_blocks = spread.shape[0] // 2
    in_group = parent_blocks // groups
    stores = []
    for g in range(groups):

        def one(k, carry):
            block = g * in_group + k
            at = source_block[col_index, block]
            value = child[pl.ds(jnp.maximum(at, 0) * 2, 2)]
            spread[pl.ds(block * 2, 2)] = jnp.where(at >= 0, value, jnp.zeros_like(value))
            return carry

        lax.fori_loop(0, in_group, one, 0)
        span = pl.ds(g * in_group * 2, in_group * 2)
        stores.append(load(spread.at[span], spread_out.at[span], spread_sem.at[g]))
    for copy in sent:
        copy.wait_send()
    for copy in stores:
        copy.wait()
    upper_done.wait()
    lower_done.wait()


def factor_update(source_block, slot_block, order, rows, inverse_lower, inverse_upper, front, devices):
    pivots = inverse_lower.shape[1]
    width = rows.shape[1]
    slots, block_rows, size = front.shape[1:]
    lanes = slots * block_rows
    piece = 64
    smem = pl.BlockSpec(memory_space=pltpu.SMEM)
    anywhere = pl.BlockSpec(memory_space=pl.ANY)
    return pl.pallas_call(
        factor_and_update,
        out_shape=(
            jax.ShapeDtypeStruct((width, pivots), jnp.bfloat16),
            jax.ShapeDtypeStruct((lanes, pivots), jnp.bfloat16),
            jax.ShapeDtypeStruct((devices, piece, lanes), jnp.bfloat16),
        ),
        in_specs=[
            smem,
            smem,
            pl.BlockSpec(memory_space=pltpu.VMEM),
            anywhere,
            anywhere,
            anywhere,
            anywhere,
        ],
        out_specs=(anywhere, anywhere, anywhere),
        scratch_shapes=[
            pltpu.VMEM((size - pivots, pivots), jnp.bfloat16),
            pltpu.VMEM(((size - pivots) // piece, piece, lanes), jnp.bfloat16),
            pltpu.VMEM((devices, piece, lanes), jnp.bfloat16),
            pltpu.VMEM((pivots, pivots), jnp.bfloat16),
            pltpu.VMEM((width, pivots), jnp.bfloat16),
            pltpu.VMEM((pivots, pivots), jnp.bfloat16),
            pltpu.VMEM((pivots, pivots), jnp.bfloat16),
            pltpu.VMEM((slots, block_rows, pivots), jnp.bfloat16),
            pltpu.VMEM((lanes, pivots), jnp.bfloat16),
            pltpu.VMEM((2, slots, block_rows, 2 * width), jnp.bfloat16),
            pltpu.SemaphoreType.DMA((60,)),
            pltpu.SemaphoreType.DMA((60,)),
            pltpu.SemaphoreType.DMA((4,)),
            pltpu.SemaphoreType.DMA((2,)),
            pltpu.SemaphoreType.DMA((2,)),
            pltpu.SemaphoreType.DMA((8,)),
        ],
        compiler_params=pltpu.CompilerParams(
            collective_id=0, has_side_effects=True, vmem_limit_bytes=58 * MIB
        ),
    )(source_block, slot_block, order, rows, inverse_lower, inverse_upper, front)


def assemble_kernel(place, arrived, initial, out):
    parent = pl.program_id(0)
    block_rows = 128
    slots = arrived.shape[3] // block_rows

    def one(block, carry):
        lanes = pl.ds(pl.multiple_of(block * block_rows, block_rows), block_rows)
        total = None
        for child in range(2):
            at = place[parent * 2 + child, block]
            safe = jnp.maximum(at, 0)
            slot_lanes = pl.ds(
                pl.multiple_of(lax.rem(safe, slots) * block_rows, block_rows), block_rows
            )
            value = arrived[lax.div(safe, slots), child, :, slot_lanes].astype(jnp.float32)
            value = jnp.where(at >= 0, value, 0.0)
            total = value if total is None else total + value
        out[0, :, lanes] = (initial[0, :, lanes].astype(jnp.float32) + total).astype(jnp.bfloat16)
        return carry

    lax.fori_loop(0, out.shape[2] // block_rows, one, 0, unroll=4)


def assemble(place, arrived, initial):
    parents, piece, order = initial.shape
    rows, fronts, _, width = arrived.shape
    return pl.pallas_call(
        assemble_kernel,
        grid=(parents,),
        out_shape=jax.ShapeDtypeStruct(initial.shape, initial.dtype),
        in_specs=[
            pl.BlockSpec(memory_space=pltpu.SMEM),
            pl.BlockSpec((rows, 2, piece, width), lambda p: (0, p, 0, 0)),
            pl.BlockSpec((1, piece, order), lambda p: (p, 0, 0)),
        ],
        out_specs=pl.BlockSpec((1, piece, order), lambda p: (p, 0, 0)),
        compiler_params=pltpu.CompilerParams(vmem_limit_bytes=48 * MIB),
    )(place, arrived, initial)


def places(slot_block, parent_map, parent_blocks):
    block_ids = jnp.arange(parent_map.shape[1], dtype=jnp.int32)
    hit = slot_block[:, :, None] == block_ids[None, None, :]
    target = jnp.sum(jnp.where(hit, parent_map[:, None, :] + 1, 0), axis=2) - 1
    parent_ids = jnp.arange(parent_blocks, dtype=jnp.int32)
    slot_ids = jnp.arange(slot_block.shape[1], dtype=jnp.int32)
    match = target[:, None, :] == parent_ids[None, :, None]
    return jnp.sum(jnp.where(match, slot_ids[None, None, :] + 1, 0), axis=2) - 1


def shards(
    pivot_rows,
    pivot_order,
    inverse_lower,
    inverse_upper,
    front_rows,
    slot_block,
    parent_map,
    parent_init,
):
    rows, cols = lax.axis_size("row"), lax.axis_size("col")
    parent_blocks = parent_init.shape[2] // front_rows.shape[2]
    parent_ids = jnp.arange(parent_blocks, dtype=jnp.int32)
    block_ids = jnp.arange(parent_map.shape[1], dtype=jnp.int32)
    hits = parent_map[:, None, :] == parent_ids[None, :, None]
    source_block = jnp.sum(jnp.where(hits, block_ids[None, None, :] + 1, 0), axis=2) - 1
    upper, lower, spread = factor_update(
        source_block,
        slot_block,
        pivot_order,
        jnp.swapaxes(pivot_rows, 1, 2),
        inverse_lower,
        inverse_upper,
        front_rows,
        rows * cols,
    )
    arrived = lax.all_to_all(spread, ("row", "col"), split_axis=0, concat_axis=0, tiled=True)
    place = places(slot_block, parent_map, parent_blocks)
    assembled = assemble(place, arrived.reshape(rows, cols, *arrived.shape[1:]), parent_init)
    return (lower.reshape(*front_rows.shape[:3], -1), upper.T[None], assembled)


def solution(mesh):
    return jax.shard_map(
        shards,
        mesh=mesh,
        in_specs=(
            P("col", None, "row"),
            P("col", None),
            P("col", None, None),
            P("col", None, None),
            P("col", "row", None, None),
            P(),
            P(),
            P(None, ("row", "col"), None),
        ),
        out_specs=(
            P("col", "row", None, None),
            P("col", None, "row"),
            P(None, ("row", "col"), None),
        ),
        check_vma=False,
    )
```

time: 274 us -> 219 us (0.80)
  waiting for transfers between devices: 202 us -> 99.3 us
  Pallas kernels: 39.3 us -> 103 us
  between operations: 14.1 us -> 0.74 us
  local copies, waits for them, and re-layouts: 9.15 us -> 4.1 us
    all_gather x1 -> x0, waiting for transfers between devices: 103 us -> none  [shards(): gathered = lax.all_gather(upper_t, 'row', axis=0, tiled=True)]
    pallas_call x2 -> x1, Pallas kernels: 31.7 us -> 95.2 us  [factor_update(): pl.pallas_call(factor_and_update, out_shape=(jax.ShapeDtypeStruct((width,...]
    unnamed x18 -> x12, local copies, waits for them, and re-layouts: 9.15 us -> 4.1 us
  transfers between devices with their start and end apart: 2 -> 1, of which waited for: 2 -> 1; matrix products, arithmetic and copies ran while one was open for 0% -> 0% of each run, Pallas kernels for 0% -> 0%
where the time goes in v2:
time: 219 us
  Pallas kernels  103 us (47%)
  waiting for transfers between devices  99.3 us (45%)
  starting transfers between devices  9.96 us (5%)
  local copies, waits for them, and re-layouts  4.1 us (2%)
    all_to_all x1, waiting for transfers between devices, shards(): lax.all_to_all(spread, ('row', 'col'), split_axis=0, concat_axis=0, tiled...  99.3 us
    pallas_call x1, Pallas kernels, factor_update(): pl.pallas_call(factor_and_update, out_shape=(jax.ShapeDtypeStruct((width,...  95.2 us
    all_to_all x1, starting transfers between devices, shards(): lax.all_to_all(spread, ('row', 'col'), split_axis=0, concat_axis=0, tiled...  9.96 us
    pallas_call x1, Pallas kernels, assemble(): pl.pallas_call(assemble_kernel, grid=(parents,), out_shape=jax.ShapeDtype...  7.78 us
  transfers between devices with their start and end apart: 1, of which 1 were waited for; matrix products, arithmetic and copies ran while one was open for 0% of the time, Pallas kernels for 0%

profile of v2, /device:TPU:15, one launch (start us, length us, event | category | flops | bytes accessed | tf_op | source)
XLA Modules:
  0.0 218.8 jit_solution(17622933962041965384)
XLA Ops:
  0.6 0.8 select_reduce_fusion.2
  1.5 0.6 broadcast_add_fusion.3.source_block
  2.1 95.2 %shard_map.103 = (bf16[448,1024]{1,0:T(8,128)(2,1)}, bf16[512,1024]{1,0:T(8,128)(2,1)}, bf16[128,64,512]{2,1,0:T(8,128)(2,1)}) custom-call(s32[8,64]{1,0:T(8,128)} %broadcast_add_fusion.3.source_block, s32[8,64]{1,0:T(8,128)} %slot_block.1, s32[1,1024]{1,0:T(1,128)} %order.1, bf16[1,448,1024]{2,1,0:T(8,128)(2,1)} %bitcast.8, ...), custom_call_target="tpu_custom_call" | custom-call | tf_op jit(solution)/shard_map/pallas_call | solution.py:288
  97.2 0.0 copy-start.4
  97.3 0.0 copy-start.3
  97.3 10.0 %all-to-all-start = ((bf16[128,64,512]{2,1,0:T(8,128)(2,1)}), bf16[128,64,512]{2,1,0:T(8,128)(2,1)}, u32[]{:S(2)}, u32[]{:S(2)}) async-start(bf16[128,64,512]{2,1,0:T(8,128)(2,1)} %get-tuple-element.8), calls=%async_computation | async-start | bytes 16777216 | tf_op jit(solution)/shard_map/all_to_all | solution.py:405
  107.2 0.0 copy-done.4
  107.3 0.0 copy-done.3
  107.3 0.1 select_reduce_fusion.1
  107.4 0.2 select_reduce_fusion
  107.7 99.3 %all-to-all-done = bf16[128,64,512]{2,1,0:T(8,128)(2,1)} async-done(((bf16[128,64,512]{2,1,0:T(8,128)(2,1)}), bf16[128,64,512]{2,1,0:T(8,128)(2,1)}, u32[]{:S(2)}, u32[]{:S(2)}) %all-to-all-start) | async-done | bytes 8388640 | tf_op jit(solution)/shard_map/all_to_all | solution.py:405
  206.9 0.0 copy-start
  206.9 2.2 copy-done
  209.1 0.0 copy-start.1
  209.1 0.0 copy-start.2
  209.1 7.8 %shard_map.104 = bf16[4,64,8192]{2,1,0:T(8,128)(2,1)} custom-call(s32[8,64]{1,0:T(8,128)S(1)} %broadcast_add_fusion.1.place, bf16[16,8,64,512]{3,2,1,0:T(8,128)(2,1)} %bitcast.4.arrived, bf16[4,64,8192]{2,1,0:T(8,128)(2,1)S(1)} %copy-done), custom_call_target="tpu_custom_call" | custom-call | tf_op jit(solution)/shard_map/pallas_call | solution.py:355
  216.9 0.0 copy-done.1
  216.9 1.0 copy.13
  217.9 0.0 copy-done.2
  217.9 0.9 copy.14
  (5 shorter events, 0.0 us)
Async XLA Ops:
  97.2 10.0 %copy-start.4 = (s32[8,56]{1,0:T(8,128)S(1)}, s32[8,56]{1,0:T(8,128)}, u32[]{:S(2)}) copy-start(s32[8,56]{1,0:T(8,128)} %param.14) | copy-start | bytes 5380
  97.3 10.0 %copy-start.3 = (s32[8,64]{1,0:T(8,128)S(1)}, s32[8,64]{1,0:T(8,128)}, u32[]{:S(2)}) copy-start(s32[8,64]{1,0:T(8,128)} %slot_block.1) | copy-start | bytes 6148
  97.3 109.7 %all-to-all-start = ((bf16[128,64,512]{2,1,0:T(8,128)(2,1)}), bf16[128,64,512]{2,1,0:T(8,128)(2,1)}, u32[]{:S(2)}, u32[]{:S(2)}) async-start(bf16[128,64,512]{2,1,0:T(8,128)(2,1)} %get-tuple-element.8), calls=%async_computation | async-start | bytes 16777216 | tf_op jit(solution)/shard_map/all_to_all | solution.py:405
  206.9 2.2 %copy-start = (bf16[4,64,8192]{2,1,0:T(8,128)(2,1)S(1)}, bf16[4,64,8192]{2,1,0:T(8,128)(2,1)}, u32[]{:S(2)}) copy-start(bf16[4,64,8192]{2,1,0:T(8,128)(2,1)} %initial.1) | copy-start | bytes 12582916
  209.1 7.8 %copy-start.1 = (bf16[512,1024]{1,0:T(8,128)(2,1)S(1)}, bf16[512,1024]{1,0:T(8,128)(2,1)}, u32[]{:S(2)}) copy-start(bf16[512,1024]{1,0:T(8,128)(2,1)} %get-tuple-element.6) | copy-start | bytes 3145732
  209.1 8.8 %copy-start.2 = (bf16[448,1024]{1,0:T(8,128)(2,1)S(1)}, bf16[448,1024]{1,0:T(8,128)(2,1)}, u32[]{:S(2)}) copy-start(bf16[448,1024]{1,0:T(8,128)(2,1)} %get-tuple-element.7) | copy-start | bytes 2752516

commit v3 on v2

v3 whole, which is shorter than its diff:
```python
import jax
import jax.numpy as jnp
from jax import lax
from jax.experimental import pallas as pl
from jax.experimental.pallas import tpu as pltpu
from jax.sharding import PartitionSpec as P

MIB = 1024 * 1024
NT = (((1,), (1,)), ((), ()))


def factor_update_exchange(
    source_block,
    slot_block,
    order,
    rows,
    inverse_lower,
    inverse_upper,
    front,
    upper_out,
    lower_out,
    arrived,
    gathered,
    child,
    spread,
    chosen,
    rows_held,
    inverse_lower_held,
    inverse_upper_held,
    lead,
    lower,
    trailing,
    send_sem,
    recv_sem,
    load_sem,
    trailing_sem,
    store_sem,
    push_sem,
    land_sem,
):
    row_index = lax.axis_index("row")
    col_index = lax.axis_index("col")
    z, x = row_index // 4, lax.rem(row_index, 4)
    y, core = col_index // 2, lax.rem(col_index, 2)
    slots, block_rows, pivots = lead.shape
    width = rows_held.shape[0]
    quarter = width // 4
    pairs, pair_width = 8, 2 * width
    pair_blocks = pair_width // block_rows
    devices, piece, lanes = spread.shape

    def at_row(dz, dx):
        return lax.rem(z + dz + 4, 4) * 4 + lax.rem(x + dx + 4, 4)

    def load(source, target, sem):
        copy = pltpu.make_async_copy(source, target, sem)
        copy.start()
        return copy

    rows_in = load(rows.at[0], rows_held, load_sem.at[0])
    inverse_lower_in = load(inverse_lower.at[0], inverse_lower_held, load_sem.at[1])
    lead_in = load(front.at[0, :, :, pl.ds(0, pivots)], lead, load_sem.at[2])
    inverse_upper_in = load(inverse_upper.at[0], inverse_upper_held, load_sem.at[3])

    def trailing_of(pair):
        start = pivots + pair * pair_width
        return pltpu.make_async_copy(
            front.at[0, :, :, pl.ds(start, pair_width)],
            trailing.at[pair % 2],
            trailing_sem.at[pair % 2],
        )

    trailing_of(0).start()
    trailing_of(1).start()

    def partner(number):
        dz, dx = number // 32, lax.rem(number // 8, 4)
        dy, dc = lax.rem(number // 2, 4), lax.rem(number, 2)
        other_col = lax.rem(y + dy, 4) * 2 + lax.rem(core + dc, 2)
        return lax.rem(z + dz, 4) * 4 + lax.rem(x + dx, 4), other_col

    barrier = pltpu.get_barrier_semaphore()

    def greet(number, carry):
        pl.semaphore_signal(
            barrier,
            inc=1,
            device_id=partner(number),
            device_id_type=pl.DeviceIdType.MESH,
        )
        return carry

    lax.fori_loop(1, devices, greet, 0)

    target = lax.broadcasted_iota(jnp.int32, (pivots, pivots), 0)
    chosen[...] = jnp.where(target == order[...], 1.0, 0.0).astype(jnp.bfloat16)
    rows_in.wait()
    inverse_lower_in.wait()

    def place(offset, part):
        start = at_row(*offset) * width + part * quarter
        return gathered.at[pl.ds(pl.multiple_of(start, 16), quarter)]

    numbers = {}
    sent = []

    def message(key, offset):
        _, part, axis, step = key
        number = numbers.setdefault(key, len(numbers))
        toward = (step, 0) if axis == 0 else (0, step)
        return pltpu.make_async_remote_copy(
            src_ref=place(offset, part),
            dst_ref=place(offset, part),
            send_sem=send_sem.at[number],
            recv_sem=recv_sem.at[number],
            device_id=(at_row(*toward), col_index),
            device_id_type=pl.DeviceIdType.MESH,
        )

    def send(offset, part, axis, step):
        seen = list(offset)
        seen[axis] -= step
        if seen[axis] == -2:
            seen[axis] = 2
        copy = message((tuple(seen), part, axis, step), offset)
        copy.start()
        sent.append(copy)

    def receive(offset, part, axis, step):
        message((offset, part, axis, step), offset).wait_recv()

    parts = ((0, 1), (2, 3))
    first = (1, 0)
    second = (0, 1)

    def offset_of(half, near, far):
        return (far, near) if half == 0 else (near, far)

    for part in (0, 2, 1, 3):
        span = pl.ds(part * quarter, quarter)
        permuted = jnp.dot(rows_held[span], chosen[...], preferred_element_type=jnp.float32)
        upper = lax.dot_general(
            permuted.astype(jnp.bfloat16),
            inverse_lower_held[...],
            NT,
            preferred_element_type=jnp.float32,
        )
        start = pl.multiple_of(row_index * width + part * quarter, 16)
        gathered[pl.ds(start, quarter)] = upper.astype(jnp.bfloat16)
        if part == 0:
            pl.semaphore_wait(barrier, devices - 1)
        half = part // 2
        for step in (1, -1):
            send((0, 0), part, first[half], step)
        for step in (1, -1):
            send((0, 0), part, second[half], step)
    own = pl.ds(pl.multiple_of(row_index * width, 16), width)
    upper_done = load(gathered.at[own], upper_out, store_sem.at[0])

    lead_in.wait()
    inverse_upper_in.wait()
    for s in range(slots):
        live = slot_block[col_index, row_index * slots + s] >= 0
        value = jnp.dot(lead[s], inverse_upper_held[...], preferred_element_type=jnp.float32)
        lower[pl.ds(s * block_rows, block_rows)] = jnp.where(live, value, 0.0).astype(jnp.bfloat16)
    lower_done = load(lower, lower_out, store_sem.at[1])

    def turn(pair):
        trailing_of(pair).wait()

        def one(b, carry):
            columns = pl.ds(pl.multiple_of(b * block_rows, block_rows), block_rows)
            held = pl.ds((pair * pair_blocks + b) * 2, 2)
            for s in range(slots):
                turned = trailing[pair % 2, s, :, columns].T
                child[held, :, pl.ds(s * block_rows, block_rows)] = turned.reshape(
                    2, piece, block_rows
                )
            return carry

        lax.fori_loop(0, pair_blocks, one, 0)
        if pair + 2 < pairs:
            trailing_of(pair + 2).start()

    def update(dz, dx):
        chunk = at_row(dz, dx)
        span = pl.ds(pl.multiple_of(chunk * width, 16), width)
        held = pl.ds(chunk * (width // piece), width // piece)
        product = lax.dot_general(
            gathered[span], lower[...], NT, preferred_element_type=jnp.float32
        ).reshape(width // piece, piece, lanes)
        child[held] = (child[held].astype(jnp.float32) - product).astype(jnp.bfloat16)

    def each():
        for k in range(2):
            for half in range(2):
                for step in (1, -1):
                    yield k, half, step, parts[half][k]

    def relay(near):
        for k, half, step, part in each():
            offset = offset_of(half, near, -step)
            receive(offset, part, second[half], step)
            if (k == 0) == (step == 1):
                send(offset, part, second[half], step)

    def finish(near):
        for k in range(2):
            for half in range(2):
                step = 1 if k == 0 else -1
                receive(offset_of(half, near, 2), parts[half][k], second[half], step)

    turn(0)
    for k, half, step, part in each():
        offset = offset_of(half, -step, 0)
        receive(offset, part, first[half], step)
        if (k == 0) == (step == 1):
            send(offset, part, first[half], step)
        for other in (1, -1):
            send(offset, part, second[half], other)
    turn(1)
    relay(0)
    turn(2)
    for k in range(2):
        for half in range(2):
            step = 1 if k == 0 else -1
            offset = offset_of(half, 2, 0)
            receive(offset, parts[half][k], first[half], step)
            for other in (1, -1):
                send(offset, parts[half][k], second[half], other)
    turn(3)
    turn(4)
    turn(5)
    relay(-1)
    turn(6)
    turn(7)
    relay(1)
    update(0, 0)
    for step in (1, -1):
        update(0, step)
        update(step, 0)
    finish(0)
    relay(2)
    for dz in (1, -1):
        for dx in (1, -1):
            update(dz, dx)
    update(0, 2)
    update(2, 0)
    finish(-1)
    finish(1)
    for step in (1, -1):
        update(step, 2)
        update(2, step)
    finish(2)
    update(2, 2)

    me = row_index * 8 + col_index

    def fill(other):
        at = source_block[col_index, other // 2]
        value = child[jnp.maximum(at, 0) * 2 + lax.rem(other, 2)]
        spread[other] = jnp.where(at >= 0, value, jnp.zeros_like(value))

    def push(number, carry):
        other = partner(lax.rem(number * 45, devices))
        to = other[0] * 8 + other[1]
        fill(to)
        pltpu.make_async_remote_copy(
            src_ref=spread.at[to],
            dst_ref=arrived.at[me],
            send_sem=push_sem,
            recv_sem=land_sem,
            device_id=other,
            device_id_type=pl.DeviceIdType.MESH,
        ).start()
        return carry

    lax.fori_loop(1, devices, push, 0)
    fill(me)
    kept = load(spread.at[me], arrived.at[me], store_sem.at[2])
    for copy in sent:
        copy.wait_send()
    upper_done.wait()
    lower_done.wait()
    kept.wait()
    others = pl.ds(0, devices - 1)
    pushed = pltpu.make_async_remote_copy(
        src_ref=spread.at[others],
        dst_ref=arrived.at[others],
        send_sem=push_sem,
        recv_sem=land_sem,
        device_id=partner(1),
        device_id_type=pl.DeviceIdType.MESH,
    )
    pushed.wait_send()
    pushed.wait_recv()


def factor_update(source_block, slot_block, order, rows, inverse_lower, inverse_upper, front, devices):
    pivots = inverse_lower.shape[1]
    width = rows.shape[1]
    slots, block_rows, size = front.shape[1:]
    lanes = slots * block_rows
    piece = 64
    smem = pl.BlockSpec(memory_space=pltpu.SMEM)
    anywhere = pl.BlockSpec(memory_space=pl.ANY)
    return pl.pallas_call(
        factor_update_exchange,
        out_shape=(
            jax.ShapeDtypeStruct((width, pivots), jnp.bfloat16),
            jax.ShapeDtypeStruct((lanes, pivots), jnp.bfloat16),
            jax.ShapeDtypeStruct((devices, piece, lanes), jnp.bfloat16),
        ),
        in_specs=[
            smem,
            smem,
            pl.BlockSpec(memory_space=pltpu.VMEM),
            anywhere,
            anywhere,
            anywhere,
            anywhere,
        ],
        out_specs=(anywhere, anywhere, anywhere),
        scratch_shapes=[
            pltpu.VMEM((size - pivots, pivots), jnp.bfloat16),
            pltpu.VMEM(((size - pivots) // piece, piece, lanes), jnp.bfloat16),
            pltpu.VMEM((devices, piece, lanes), jnp.bfloat16),
            pltpu.VMEM((pivots, pivots), jnp.bfloat16),
            pltpu.VMEM((width, pivots), jnp.bfloat16),
            pltpu.VMEM((pivots, pivots), jnp.bfloat16),
            pltpu.VMEM((pivots, pivots), jnp.bfloat16),
            pltpu.VMEM((slots, block_rows, pivots), jnp.bfloat16),
            pltpu.VMEM((lanes, pivots), jnp.bfloat16),
            pltpu.VMEM((2, slots, block_rows, 2 * width), jnp.bfloat16),
            pltpu.SemaphoreType.DMA((60,)),
            pltpu.SemaphoreType.DMA((60,)),
            pltpu.SemaphoreType.DMA((4,)),
            pltpu.SemaphoreType.DMA((2,)),
            pltpu.SemaphoreType.DMA((3,)),
            pltpu.SemaphoreType.DMA,
            pltpu.SemaphoreType.DMA,
        ],
        compiler_params=pltpu.CompilerParams(
            collective_id=0, has_side_effects=True, vmem_limit_bytes=58 * MIB
        ),
    )(source_block, slot_block, order, rows, inverse_lower, inverse_upper, front)


def assemble_kernel(place, arrived, initial, upper, lower, out, upper_out, lower_out):
    parent = pl.program_id(0)
    block_rows = 128
    slots = arrived.shape[3] // block_rows
    upper_out[...] = upper[...]
    lower_out[...] = lower[...]

    def one(block, carry):
        lanes = pl.ds(pl.multiple_of(block * block_rows, block_rows), block_rows)
        total = initial[0, :, lanes].astype(jnp.float32)
        for child in range(2):
            at = place[parent * 2 + child, block]
            safe = jnp.maximum(at, 0)
            row = lax.shift_right_logical(safe, 2)
            slot = lax.bitwise_and(safe, slots - 1)
            slot_lanes = pl.ds(pl.multiple_of(slot * block_rows, block_rows), block_rows)
            value = arrived[row, child, :, slot_lanes].astype(jnp.float32)
            total += jnp.where(at >= 0, value, 0.0)
        out[0, :, lanes] = total.astype(jnp.bfloat16)
        return carry

    lax.fori_loop(0, out.shape[2] // block_rows, one, 0, unroll=8)


def assemble(place, arrived, initial, upper, lower):
    parents, piece, order = initial.shape
    rows, _, _, width = arrived.shape
    part = lambda array: pl.BlockSpec(
        (array.shape[0] // parents, array.shape[1]), lambda p: (p, 0)
    )
    return pl.pallas_call(
        assemble_kernel,
        grid=(parents,),
        out_shape=(
            jax.ShapeDtypeStruct(initial.shape, initial.dtype),
            jax.ShapeDtypeStruct(upper.shape, upper.dtype),
            jax.ShapeDtypeStruct(lower.shape, lower.dtype),
        ),
        in_specs=[
            pl.BlockSpec(memory_space=pltpu.SMEM),
            pl.BlockSpec((rows, 2, piece, width), lambda p: (0, p, 0, 0)),
            pl.BlockSpec((1, piece, order), lambda p: (p, 0, 0)),
            part(upper),
            part(lower),
        ],
        out_specs=(
            pl.BlockSpec((1, piece, order), lambda p: (p, 0, 0)),
            part(upper),
            part(lower),
        ),
        compiler_params=pltpu.CompilerParams(vmem_limit_bytes=58 * MIB),
    )(place, arrived, initial, upper, lower)


def places(slot_block, parent_map, parent_blocks):
    block_ids = jnp.arange(parent_map.shape[1], dtype=jnp.int32)
    hit = slot_block[:, :, None] == block_ids[None, None, :]
    target = jnp.sum(jnp.where(hit, parent_map[:, None, :] + 1, 0), axis=2) - 1
    parent_ids = jnp.arange(parent_blocks, dtype=jnp.int32)
    slot_ids = jnp.arange(slot_block.shape[1], dtype=jnp.int32)
    match = target[:, None, :] == parent_ids[None, :, None]
    return jnp.sum(jnp.where(match, slot_ids[None, None, :] + 1, 0), axis=2) - 1


def shards(
    pivot_rows,
    pivot_order,
    inverse_lower,
    inverse_upper,
    front_rows,
    slot_block,
    parent_map,
    parent_init,
):
    rows, cols = lax.axis_size("row"), lax.axis_size("col")
    parent_blocks = parent_init.shape[2] // front_rows.shape[2]
    parent_ids = jnp.arange(parent_blocks, dtype=jnp.int32)
    block_ids = jnp.arange(parent_map.shape[1], dtype=jnp.int32)
    hits = parent_map[:, None, :] == parent_ids[None, :, None]
    source_block = jnp.sum(jnp.where(hits, block_ids[None, None, :] + 1, 0), axis=2) - 1
    upper, lower, arrived = factor_update(
        source_block,
        slot_block,
        pivot_order,
        jnp.swapaxes(pivot_rows, 1, 2),
        inverse_lower,
        inverse_upper,
        front_rows,
        rows * cols,
    )
    place = places(slot_block, parent_map, parent_blocks)
    assembled, upper, lower = assemble(
        place, arrived.reshape(rows, cols, *arrived.shape[1:]), parent_init, upper, lower
    )
    return (lower.reshape(*front_rows.shape[:3], -1), upper.T[None], assembled)


def solution(mesh):
    return jax.shard_map(
        shards,
        mesh=mesh,
        in_specs=(
            P("col", None, "row"),
            P("col", None),
            P("col", None, None),
            P("col", None, None),
            P("col", "row", None, None),
            P(),
            P(),
            P(None, ("row", "col"), None),
        ),
        out_specs=(
            P("col", "row", None, None),
            P("col", None, "row"),
            P(None, ("row", "col"), None),
        ),
        check_vma=False,
    )
```

time: 219 us -> 212 us (0.968)
  the two profiles are of different devices: /device:TPU:15 before, /device:TPU:13 now
where the time goes in v3:
time: 212 us
  Pallas kernels  208 us (98%)
  other arithmetic  3.76 us (2%)
    pallas_call x1, Pallas kernels, factor_update(): pl.pallas_call(factor_update_exchange, out_shape=(jax.ShapeDtypeStruct((w...  198 us
    pallas_call x1, Pallas kernels, assemble(): pl.pallas_call(assemble_kernel, grid=(parents,), out_shape=(jax.ShapeDtyp...  9.31 us

profile of v3, /device:TPU:13, one launch (start us, length us, event | category | flops | bytes accessed | tf_op | source)
XLA Modules:
  0.0 212.1 jit_solution(12992341046559666648)
XLA Ops:
  0.7 0.8 select_reduce_fusion.1
  1.5 0.6 broadcast_add_fusion.source_block
  2.1 0.7 broadcast_add_fusion.3
  2.8 0.8 select_reduce_fusion.2
  3.6 0.2 select_reduce_fusion
  3.8 0.6 broadcast_add_fusion.1.place
  4.4 198.3 %shard_map.103 = (bf16[448,1024]{1,0:T(8,128)(2,1)}, bf16[512,1024]{1,0:T(8,128)(2,1)}, bf16[128,64,512]{2,1,0:T(8,128)(2,1)}) custom-call(s32[8,64]{1,0:T(8,128)} %broadcast_add_fusion.source_block, s32[8,64]{1,0:T(8,128)} %slot_block.1, s32[1,1024]{1,0:T(1,128)} %order.1, bf16[1,448,1024]{2,1,0:T(8,128)(2,1)} %bitcast.7, ...), custom_call_target="tpu_custom_call" | custom-call | tf_op jit(solution)/shard_map/pallas_call | solution.py:307
  202.7 9.3 %shard_map.104 = (bf16[4,64,8192]{2,1,0:T(8,128)(2,1)}, bf16[448,1024]{1,0:T(8,128)(2,1)}, bf16[512,1024]{1,0:T(8,128)(2,1)}) custom-call(s32[8,64]{1,0:T(8,128)} %broadcast_add_fusion.1.place, bf16[16,8,64,512]{3,2,1,0:T(8,128)(2,1)} %bitcast.6, bf16[4,64,8192]{2,1,0:T(8,128)(2,1)} %initial.1, bf16[448,1024]{1,0:T(8,128)(2,1)} %get-tuple-element.10.upper, ...), custom_call_target="tpu_custom_call" | custom-call | tf_op jit(solution)/shard_map/pallas_call | solution.py:379
  (3 shorter events, 0.0 us)

commit v4 on v3

--- a/solution.py
+++ b/solution.py
@@ -59,8 +59,6 @@
 
     rows_in = load(rows.at[0], rows_held, load_sem.at[0])
     inverse_lower_in = load(inverse_lower.at[0], inverse_lower_held, load_sem.at[1])
-    lead_in = load(front.at[0, :, :, pl.ds(0, pivots)], lead, load_sem.at[2])
-    inverse_upper_in = load(inverse_upper.at[0], inverse_upper_held, load_sem.at[3])
 
     def trailing_of(pair):
         start = pivots + pair * pair_width
@@ -70,9 +68,6 @@
             trailing_sem.at[pair % 2],
         )
 
-    trailing_of(0).start()
-    trailing_of(1).start()
-
     def partner(number):
         dz, dx = number // 32, lax.rem(number // 8, 4)
         dy, dc = lax.rem(number // 2, 4), lax.rem(number, 2)
@@ -81,21 +76,21 @@
 
     barrier = pltpu.get_barrier_semaphore()
 
-    def greet(number, carry):
+    near = [(at_row(dz, dx), col_index) for dz, dx in ((0, 1), (0, -1), (1, 0), (-1, 0))]
+    across = [(row_index, partner(number)[1]) for number in range(1, 8)]
+    for other in near + across:
         pl.semaphore_signal(
-            barrier,
-            inc=1,
-            device_id=partner(number),
-            device_id_type=pl.DeviceIdType.MESH,
+            barrier, inc=1, device_id=other, device_id_type=pl.DeviceIdType.MESH
         )
-        return carry
-
-    lax.fori_loop(1, devices, greet, 0)
 
     target = lax.broadcasted_iota(jnp.int32, (pivots, pivots), 0)
     chosen[...] = jnp.where(target == order[...], 1.0, 0.0).astype(jnp.bfloat16)
     rows_in.wait()
     inverse_lower_in.wait()
+    lead_in = load(front.at[0, :, :, pl.ds(0, pivots)], lead, load_sem.at[2])
+    inverse_upper_in = load(inverse_upper.at[0], inverse_upper_held, load_sem.at[3])
+    trailing_of(0).start()
+    trailing_of(1).start()
 
     def place(offset, part):
         start = at_row(*offset) * width + part * quarter
@@ -148,7 +143,7 @@
         start = pl.multiple_of(row_index * width + part * quarter, 16)
         gathered[pl.ds(start, quarter)] = upper.astype(jnp.bfloat16)
         if part == 0:
-            pl.semaphore_wait(barrier, devices - 1)
+            pl.semaphore_wait(barrier, len(near + across))
         half = part // 2
         for step in (1, -1):
             send((0, 0), part, first[half], step)
@@ -165,6 +160,8 @@
         lower[pl.ds(s * block_rows, block_rows)] = jnp.where(live, value, 0.0).astype(jnp.bfloat16)
     lower_done = load(lower, lower_out, store_sem.at[1])
 
+    live = [slot_block[col_index, row_index * slots + s] >= 0 for s in range(slots)]
+
     def turn(pair):
         trailing_of(pair).wait()
 
@@ -173,6 +170,7 @@
             held = pl.ds((pair * pair_blocks + b) * 2, 2)
             for s in range(slots):
                 turned = trailing[pair % 2, s, :, columns].T
+                turned = jnp.where(live[s], turned, jnp.zeros_like(turned))
                 child[held, :, pl.ds(s * block_rows, block_rows)] = turned.reshape(
                     2, piece, block_rows
                 )
@@ -353,21 +351,27 @@
     upper_out[...] = upper[...]
     lower_out[...] = lower[...]
 
-    def one(block, carry):
-        lanes = pl.ds(pl.multiple_of(block * block_rows, block_rows), block_rows)
-        total = initial[0, :, lanes].astype(jnp.float32)
-        for child in range(2):
-            at = place[parent * 2 + child, block]
-            safe = jnp.maximum(at, 0)
-            row = lax.shift_right_logical(safe, 2)
-            slot = lax.bitwise_and(safe, slots - 1)
-            slot_lanes = pl.ds(pl.multiple_of(slot * block_rows, block_rows), block_rows)
-            value = arrived[row, child, :, slot_lanes].astype(jnp.float32)
-            total += jnp.where(at >= 0, value, 0.0)
-        out[0, :, lanes] = total.astype(jnp.bfloat16)
+    together = 4
+
+    def some(step, carry):
+        blocks = [step * together + k for k in range(together)]
+        at = [pl.ds(pl.multiple_of(b * block_rows, block_rows), block_rows) for b in blocks]
+        held = []
+        for b, lanes in zip(blocks, at):
+            terms = [initial[0, :, lanes]]
+            for child in range(2):
+                source = place[parent * 2 + child, b]
+                row = lax.shift_right_logical(source, 2)
+                slot = lax.bitwise_and(source, slots - 1)
+                slot_lanes = pl.ds(pl.multiple_of(slot * block_rows, block_rows), block_rows)
+                terms.append(arrived[row, child, :, slot_lanes])
+            held.append(terms)
+        for lanes, (first, left, right) in zip(at, held):
+            total = left.astype(jnp.float32) + right.astype(jnp.float32)
+            out[0, :, lanes] = (first.astype(jnp.float32) + total).astype(jnp.bfloat16)
         return carry
 
-    lax.fori_loop(0, out.shape[2] // block_rows, one, 0, unroll=8)
+    lax.fori_loop(0, out.shape[2] // block_rows // together, some, 0, unroll=2)
 
 
 def assemble(place, arrived, initial, upper, lower):
@@ -407,7 +411,9 @@
     parent_ids = jnp.arange(parent_blocks, dtype=jnp.int32)
     slot_ids = jnp.arange(slot_block.shape[1], dtype=jnp.int32)
     match = target[:, None, :] == parent_ids[None, :, None]
-    return jnp.sum(jnp.where(match, slot_ids[None, None, :] + 1, 0), axis=2) - 1
+    empty = jnp.max(jnp.where(slot_block < 0, slot_ids[None, :], 0), axis=1)
+    held = jnp.sum(jnp.where(match, slot_ids[None, None, :] + 1, 0), axis=2)
+    return jnp.where(held > 0, held - 1, empty[:, None])
 
 
 def shards(

time: 212 us -> 200 us (0.943)
  the two profiles are of different devices: /device:TPU:13 before, /device:TPU:15 now
where the time goes in v4:
time: 200 us; the launch traced here: 199 us
  Pallas kernels  194 us (97%)
  other arithmetic  4.63 us (2%)
    pallas_call x1, Pallas kernels, factor_update(): pl.pallas_call(factor_update_exchange, out_shape=(jax.ShapeDtypeStruct((w...  185 us
    pallas_call x1, Pallas kernels, assemble(): pl.pallas_call(assemble_kernel, grid=(parents,), out_shape=(jax.ShapeDtyp...  8.95 us

profile of v4, /device:TPU:15, one launch (start us, length us, event | category | flops | bytes accessed | tf_op | source)
XLA Modules:
  0.0 199.3 jit_solution(18175283716992919587)
XLA Ops:
  0.6 0.8 select_reduce_fusion.3
  1.5 0.8 select_reduce_fusion.1
  2.3 0.6 broadcast_add_fusion.source_block
  2.9 0.7 broadcast_add_fusion.2
  3.6 0.8 select_reduce_fusion.2
  4.4 0.2 select_reduce_fusion
  4.6 0.7 add_select_fusion.place
  5.3 185.0 %shard_map.103 = (bf16[448,1024]{1,0:T(8,128)(2,1)}, bf16[512,1024]{1,0:T(8,128)(2,1)}, bf16[128,64,512]{2,1,0:T(8,128)(2,1)}) custom-call(s32[8,64]{1,0:T(8,128)} %broadcast_add_fusion.source_block, s32[8,64]{1,0:T(8,128)} %slot_block.1, s32[1,1024]{1,0:T(1,128)} %order.1, bf16[1,448,1024]{2,1,0:T(8,128)(2,1)} %bitcast.7, ...), custom_call_target="tpu_custom_call" | custom-call | tf_op jit(solution)/shard_map/pallas_call | solution.py:305
  190.3 8.9 %shard_map.104 = (bf16[4,64,8192]{2,1,0:T(8,128)(2,1)}, bf16[448,1024]{1,0:T(8,128)(2,1)}, bf16[512,1024]{1,0:T(8,128)(2,1)}) custom-call(s32[8,64]{1,0:T(8,128)} %add_select_fusion.place, bf16[16,8,64,512]{3,2,1,0:T(8,128)(2,1)} %bitcast.6, bf16[4,64,8192]{2,1,0:T(8,128)(2,1)} %initial.1, bf16[448,1024]{1,0:T(8,128)(2,1)} %get-tuple-element.10.upper, ...), custom_call_target="tpu_custom_call" | custom-call | tf_op jit(solution)/shard_map/pallas_call | solution.py:383
  (3 shorter events, 0.0 us)

commit v5 on v4

--- a/solution.py
+++ b/solution.py
@@ -9,9 +9,38 @@
 NT = (((1,), (1,)), ((), ()))
 
 
+def column_of(row):
+    count = row.shape[1]
+    down = lax.broadcasted_iota(jnp.int32, (count, count), 0)
+    along = lax.broadcasted_iota(jnp.int32, (count, count), 1)
+    return jnp.sum(jnp.where(down == along, row, 0), axis=1, keepdims=True)
+
+
+def place_row(slots, targets, width):
+    count, blocks = slots.shape[1], targets.shape[1]
+    block_ids = lax.broadcasted_iota(jnp.int32, (count, blocks), 1)
+    hit = column_of(slots) == block_ids
+    target = jnp.max(jnp.where(hit, targets, -1), axis=1, keepdims=True)
+    parent_ids = lax.broadcasted_iota(jnp.int32, (count, width), 1)
+    slot_ids = lax.broadcasted_iota(jnp.int32, (count, width), 0)
+    held = jnp.max(jnp.where(target == parent_ids, slot_ids, -1), axis=0, keepdims=True)
+    along = lax.broadcasted_iota(jnp.int32, slots.shape, 1)
+    empty = jnp.max(jnp.where(slots < 0, along, 0), axis=1, keepdims=True)
+    return jnp.where(held >= 0, held, empty)
+
+
+def source_row(targets, width):
+    blocks = targets.shape[1]
+    parent_ids = lax.broadcasted_iota(jnp.int32, (blocks, width), 1)
+    block_ids = lax.broadcasted_iota(jnp.int32, (blocks, width), 0)
+    hit = column_of(targets) == parent_ids
+    return jnp.max(jnp.where(hit, block_ids, -1), axis=0, keepdims=True)
+
+
 def factor_update_exchange(
-    source_block,
     slot_block,
+    slot_rows,
+    parent_map,
     order,
     rows,
     inverse_lower,
@@ -20,6 +49,7 @@
     upper_out,
     lower_out,
     arrived,
+    table_out,
     gathered,
     child,
     spread,
@@ -30,6 +60,8 @@
     lead,
     lower,
     trailing,
+    table,
+    source,
     send_sem,
     recv_sem,
     load_sem,
@@ -232,6 +264,13 @@
     relay(-1)
     turn(6)
     turn(7)
+    fronts, columns = slot_rows.shape[0], table.shape[1]
+    for f in range(fronts):
+        table[f : f + 1] = place_row(slot_rows[f : f + 1], parent_map[f : f + 1], columns)
+    own_map = parent_map[pl.ds(col_index, 1)]
+    table[fronts : fronts + 1] = source_row(own_map, columns)
+    table_done = load(table, table_out, store_sem.at[3])
+    source_done = load(table, source, store_sem.at[4])
     relay(1)
     update(0, 0)
     for step in (1, -1):
@@ -253,14 +292,15 @@
     update(2, 2)
 
     me = row_index * 8 + col_index
+    source_done.wait()
 
     def fill(other):
-        at = source_block[col_index, other // 2]
+        at = source[fronts, other // 2]
         value = child[jnp.maximum(at, 0) * 2 + lax.rem(other, 2)]
         spread[other] = jnp.where(at >= 0, value, jnp.zeros_like(value))
 
     def push(number, carry):
-        other = partner(lax.rem(number * 45, devices))
+        other = partner(lax.rem(number * 109, devices))
         to = other[0] * 8 + other[1]
         fill(to)
         pltpu.make_async_remote_copy(
@@ -280,6 +320,7 @@
         copy.wait_send()
     upper_done.wait()
     lower_done.wait()
+    table_done.wait()
     kept.wait()
     others = pl.ds(0, devices - 1)
     pushed = pltpu.make_async_remote_copy(
@@ -294,13 +335,15 @@
     pushed.wait_recv()
 
 
-def factor_update(source_block, slot_block, order, rows, inverse_lower, inverse_upper, front, devices):
+def factor_update(slot_block, parent_map, order, rows, inverse_lower, inverse_upper, front, devices):
     pivots = inverse_lower.shape[1]
     width = rows.shape[1]
     slots, block_rows, size = front.shape[1:]
     lanes = slots * block_rows
     piece = 64
+    table = (16, 128)
     smem = pl.BlockSpec(memory_space=pltpu.SMEM)
+    vmem = pl.BlockSpec(memory_space=pltpu.VMEM)
     anywhere = pl.BlockSpec(memory_space=pl.ANY)
     return pl.pallas_call(
         factor_update_exchange,
@@ -308,17 +351,19 @@
             jax.ShapeDtypeStruct((width, pivots), jnp.bfloat16),
             jax.ShapeDtypeStruct((lanes, pivots), jnp.bfloat16),
             jax.ShapeDtypeStruct((devices, piece, lanes), jnp.bfloat16),
+            jax.ShapeDtypeStruct(table, jnp.int32),
         ),
         in_specs=[
             smem,
-            smem,
-            pl.BlockSpec(memory_space=pltpu.VMEM),
+            vmem,
+            vmem,
+            vmem,
             anywhere,
             anywhere,
             anywhere,
             anywhere,
         ],
-        out_specs=(anywhere, anywhere, anywhere),
+        out_specs=(anywhere, anywhere, anywhere, anywhere),
         scratch_shapes=[
             pltpu.VMEM((size - pivots, pivots), jnp.bfloat16),
             pltpu.VMEM(((size - pivots) // piece, piece, lanes), jnp.bfloat16),
@@ -330,18 +375,20 @@
             pltpu.VMEM((slots, block_rows, pivots), jnp.bfloat16),
             pltpu.VMEM((lanes, pivots), jnp.bfloat16),
             pltpu.VMEM((2, slots, block_rows, 2 * width), jnp.bfloat16),
+            pltpu.VMEM(table, jnp.int32),
+            pltpu.SMEM(table, jnp.int32),
             pltpu.SemaphoreType.DMA((60,)),
             pltpu.SemaphoreType.DMA((60,)),
             pltpu.SemaphoreType.DMA((4,)),
             pltpu.SemaphoreType.DMA((2,)),
-            pltpu.SemaphoreType.DMA((3,)),
+            pltpu.SemaphoreType.DMA((5,)),
             pltpu.SemaphoreType.DMA,
             pltpu.SemaphoreType.DMA,
         ],
         compiler_params=pltpu.CompilerParams(
             collective_id=0, has_side_effects=True, vmem_limit_bytes=58 * MIB
         ),
-    )(source_block, slot_block, order, rows, inverse_lower, inverse_upper, front)
+    )(slot_block, slot_block, parent_map, order, rows, inverse_lower, inverse_upper, front)
 
 
 def assemble_kernel(place, arrived, initial, upper, lower, out, upper_out, lower_out):
@@ -404,18 +451,6 @@
     )(place, arrived, initial, upper, lower)
 
 
-def places(slot_block, parent_map, parent_blocks):
-    block_ids = jnp.arange(parent_map.shape[1], dtype=jnp.int32)
-    hit = slot_block[:, :, None] == block_ids[None, None, :]
-    target = jnp.sum(jnp.where(hit, parent_map[:, None, :] + 1, 0), axis=2) - 1
-    parent_ids = jnp.arange(parent_blocks, dtype=jnp.int32)
-    slot_ids = jnp.arange(slot_block.shape[1], dtype=jnp.int32)
-    match = target[:, None, :] == parent_ids[None, :, None]
-    empty = jnp.max(jnp.where(slot_block < 0, slot_ids[None, :], 0), axis=1)
-    held = jnp.sum(jnp.where(match, slot_ids[None, None, :] + 1, 0), axis=2)
-    return jnp.where(held > 0, held - 1, empty[:, None])
-
-
 def shards(
     pivot_rows,
     pivot_order,
@@ -427,14 +462,9 @@
     parent_init,
 ):
     rows, cols = lax.axis_size("row"), lax.axis_size("col")
-    parent_blocks = parent_init.shape[2] // front_rows.shape[2]
-    parent_ids = jnp.arange(parent_blocks, dtype=jnp.int32)
-    block_ids = jnp.arange(parent_map.shape[1], dtype=jnp.int32)
-    hits = parent_map[:, None, :] == parent_ids[None, :, None]
-    source_block = jnp.sum(jnp.where(hits, block_ids[None, None, :] + 1, 0), axis=2) - 1
-    upper, lower, arrived = factor_update(
-        source_block,
+    upper, lower, arrived, place = factor_update(
         slot_block,
+        parent_map,
         pivot_order,
         jnp.swapaxes(pivot_rows, 1, 2),
         inverse_lower,
@@ -442,7 +472,6 @@
         front_rows,
         rows * cols,
     )
-    place = places(slot_block, parent_map, parent_blocks)
     assembled, upper, lower = assemble(
         place, arrived.reshape(rows, cols, *arrived.shape[1:]), parent_init, upper, lower
     )

time: 200 us -> 192 us (0.960)
  Pallas kernels: 194 us -> 189 us
  other arithmetic: 4.63 us -> 0 us
    pallas_call x1, Pallas kernels: 185 us -> 180 us  [factor_update(): pl.pallas_call(factor_update_exchange, out_shape=(jax.ShapeDtypeStruct((w...]
where the time goes in v5:
time: 192 us; the launch traced here: 190 us
  Pallas kernels  189 us (98%)
    pallas_call x1, Pallas kernels, factor_update(): pl.pallas_call(factor_update_exchange, out_shape=(jax.ShapeDtypeStruct((w...  180 us
    pallas_call x1, Pallas kernels, assemble(): pl.pallas_call(assemble_kernel, grid=(parents,), out_shape=(jax.ShapeDtyp...  8.95 us

profile of v5, /device:TPU:15, one launch (start us, length us, event | category | flops | bytes accessed | tf_op | source)
XLA Modules:
  0.0 189.8 jit_solution(1886419963584589916)
XLA Ops:
  0.6 180.2 %shard_map.103 = (bf16[448,1024]{1,0:T(8,128)(2,1)}, bf16[512,1024]{1,0:T(8,128)(2,1)}, bf16[128,64,512]{2,1,0:T(8,128)(2,1)}, s32[16,128]{1,0:T(8,128)}) custom-call(s32[8,64]{1,0:T(8,128)} %slot_rows.1, s32[8,64]{1,0:T(8,128)} %slot_rows.1, s32[8,56]{1,0:T(8,128)} %parent_map.1, s32[1,1024]{1,0:T(1,128)} %order.1, bf16[1,448,1024]{2,1,0:T(8,128)(2,1)} %bitcast.7, ...), custom_call_target="tpu_custom_call" | custom-call | tf_op jit(solution)/shard_map/pallas_call | solution.py:348
  180.9 8.9 %shard_map.104 = (bf16[4,64,8192]{2,1,0:T(8,128)(2,1)}, bf16[448,1024]{1,0:T(8,128)(2,1)}, bf16[512,1024]{1,0:T(8,128)(2,1)}) custom-call(s32[16,128]{1,0:T(8,128)} %get-tuple-element.10.place, bf16[16,8,64,512]{3,2,1,0:T(8,128)(2,1)} %bitcast.6, bf16[4,64,8192]{2,1,0:T(8,128)(2,1)} %initial.1, bf16[448,1024]{1,0:T(8,128)(2,1)} %get-tuple-element.12.upper, ...), custom_call_target="tpu_custom_call" | custom-call | tf_op jit(solution)/shard_map/pallas_call | solution.py:430

commit v6 on v5

--- a/solution.py
+++ b/solution.py
@@ -7,6 +7,10 @@
 
 MIB = 1024 * 1024
 NT = (((1,), (1,)), ((), ()))
+
+
+def in_hbm(array):
+    return pltpu.with_memory_space_constraint(array, pltpu.HBM)
 
 
 def column_of(row):
@@ -39,9 +43,9 @@
 
 def factor_update_exchange(
     slot_block,
-    slot_rows,
-    parent_map,
-    order,
+    slot_rows_in,
+    parent_map_in,
+    order_in,
     rows,
     inverse_lower,
     inverse_upper,
@@ -61,6 +65,9 @@
     lower,
     trailing,
     table,
+    slot_rows,
+    parent_map,
+    order,
     source,
     send_sem,
     recv_sem,
@@ -89,6 +96,11 @@
         copy.start()
         return copy
 
+    small = [
+        load(order_in, order, load_sem.at[4]),
+        load(slot_rows_in, slot_rows, load_sem.at[5]),
+        load(parent_map_in, parent_map, load_sem.at[6]),
+    ]
     rows_in = load(rows.at[0], rows_held, load_sem.at[0])
     inverse_lower_in = load(inverse_lower.at[0], inverse_lower_held, load_sem.at[1])
 
@@ -116,6 +128,8 @@
         )
 
     target = lax.broadcasted_iota(jnp.int32, (pivots, pivots), 0)
+    for copy in small:
+        copy.wait()
     chosen[...] = jnp.where(target == order[...], 1.0, 0.0).astype(jnp.bfloat16)
     rows_in.wait()
     inverse_lower_in.wait()
@@ -343,27 +357,32 @@
     piece = 64
     table = (16, 128)
     smem = pl.BlockSpec(memory_space=pltpu.SMEM)
-    vmem = pl.BlockSpec(memory_space=pltpu.VMEM)
     anywhere = pl.BlockSpec(memory_space=pl.ANY)
+    operands = (slot_block, parent_map, order, rows, inverse_lower, inverse_upper, front)
     return pl.pallas_call(
         factor_update_exchange,
         out_shape=(
             jax.ShapeDtypeStruct((width, pivots), jnp.bfloat16),
             jax.ShapeDtypeStruct((lanes, pivots), jnp.bfloat16),
-            jax.ShapeDtypeStruct((devices, piece, lanes), jnp.bfloat16),
+            pltpu.VMEM((devices, piece, lanes), jnp.bfloat16),
             jax.ShapeDtypeStruct(table, jnp.int32),
         ),
         in_specs=[
             smem,
-            vmem,
-            vmem,
-            vmem,
+            anywhere,
+            anywhere,
+            anywhere,
             anywhere,
             anywhere,
             anywhere,
             anywhere,
         ],
-        out_specs=(anywhere, anywhere, anywhere, anywhere),
+        out_specs=(
+            anywhere,
+            anywhere,
+            pl.BlockSpec(memory_space=pltpu.VMEM),
+            anywhere,
+        ),
         scratch_shapes=[
             pltpu.VMEM((size - pivots, pivots), jnp.bfloat16),
             pltpu.VMEM(((size - pivots) // piece, piece, lanes), jnp.bfloat16),
@@ -376,78 +395,92 @@
             pltpu.VMEM((lanes, pivots), jnp.bfloat16),
             pltpu.VMEM((2, slots, block_rows, 2 * width), jnp.bfloat16),
             pltpu.VMEM(table, jnp.int32),
+            pltpu.VMEM(slot_block.shape, jnp.int32),
+            pltpu.VMEM(parent_map.shape, jnp.int32),
+            pltpu.VMEM(order.shape, jnp.int32),
             pltpu.SMEM(table, jnp.int32),
             pltpu.SemaphoreType.DMA((60,)),
             pltpu.SemaphoreType.DMA((60,)),
-            pltpu.SemaphoreType.DMA((4,)),
+            pltpu.SemaphoreType.DMA((7,)),
             pltpu.SemaphoreType.DMA((2,)),
             pltpu.SemaphoreType.DMA((5,)),
             pltpu.SemaphoreType.DMA,
             pltpu.SemaphoreType.DMA,
         ],
         compiler_params=pltpu.CompilerParams(
-            collective_id=0, has_side_effects=True, vmem_limit_bytes=58 * MIB
+            collective_id=0, has_side_effects=True, vmem_limit_bytes=43 * MIB
         ),
-    )(slot_block, slot_block, parent_map, order, rows, inverse_lower, inverse_upper, front)
-
-
-def assemble_kernel(place, arrived, initial, upper, lower, out, upper_out, lower_out):
-    parent = pl.program_id(0)
+    )(slot_block, *map(in_hbm, operands))
+
+
+def assemble_kernel(
+    place,
+    arrived,
+    initial,
+    upper,
+    lower,
+    out,
+    upper_out,
+    lower_out,
+    total,
+    store_sem,
+):
+    parents, _, order = initial.shape
     block_rows = 128
     slots = arrived.shape[3] // block_rows
-    upper_out[...] = upper[...]
-    lower_out[...] = lower[...]
-
+    stores = [
+        pltpu.make_async_copy(upper, upper_out, store_sem.at[parents]),
+        pltpu.make_async_copy(lower, lower_out, store_sem.at[parents + 1]),
+    ]
+    for copy in stores:
+        copy.start()
     together = 4
-
-    def some(step, carry):
-        blocks = [step * together + k for k in range(together)]
-        at = [pl.ds(pl.multiple_of(b * block_rows, block_rows), block_rows) for b in blocks]
-        held = []
-        for b, lanes in zip(blocks, at):
-            terms = [initial[0, :, lanes]]
-            for child in range(2):
-                source = place[parent * 2 + child, b]
-                row = lax.shift_right_logical(source, 2)
-                slot = lax.bitwise_and(source, slots - 1)
-                slot_lanes = pl.ds(pl.multiple_of(slot * block_rows, block_rows), block_rows)
-                terms.append(arrived[row, child, :, slot_lanes])
-            held.append(terms)
-        for lanes, (first, left, right) in zip(at, held):
-            total = left.astype(jnp.float32) + right.astype(jnp.float32)
-            out[0, :, lanes] = (first.astype(jnp.float32) + total).astype(jnp.bfloat16)
-        return carry
-
-    lax.fori_loop(0, out.shape[2] // block_rows // together, some, 0, unroll=2)
+    for parent in range(parents):
+
+        def some(step, carry):
+            blocks = [step * together + k for k in range(together)]
+            at = [pl.ds(pl.multiple_of(b * block_rows, block_rows), block_rows) for b in blocks]
+            terms = []
+            for b, lanes in zip(blocks, at):
+                term = [initial[parent, :, lanes]]
+                for child in range(2):
+                    source = place[parent * 2 + child, b]
+                    row = lax.shift_right_logical(source, 2)
+                    slot = lax.bitwise_and(source, slots - 1)
+                    slot_lanes = pl.ds(pl.multiple_of(slot * block_rows, block_rows), block_rows)
+                    term.append(arrived[row, 2 * parent + child, :, slot_lanes])
+                terms.append(term)
+            for lanes, (first, left, right) in zip(at, terms):
+                both = left.astype(jnp.float32) + right.astype(jnp.float32)
+                total[parent, :, lanes] = (first.astype(jnp.float32) + both).astype(jnp.bfloat16)
+            return carry
+
+        lax.fori_loop(0, order // block_rows // together, some, 0, unroll=2)
+        store = pltpu.make_async_copy(total.at[parent], out.at[parent], store_sem.at[parent])
+        store.start()
+        stores.append(store)
+    for copy in stores:
+        copy.wait()
 
 
 def assemble(place, arrived, initial, upper, lower):
-    parents, piece, order = initial.shape
-    rows, _, _, width = arrived.shape
-    part = lambda array: pl.BlockSpec(
-        (array.shape[0] // parents, array.shape[1]), lambda p: (p, 0)
-    )
+    parents = initial.shape[0]
+    anywhere = pl.BlockSpec(memory_space=pl.ANY)
+    vmem = pl.BlockSpec(memory_space=pltpu.VMEM)
     return pl.pallas_call(
         assemble_kernel,
-        grid=(parents,),
         out_shape=(
             jax.ShapeDtypeStruct(initial.shape, initial.dtype),
             jax.ShapeDtypeStruct(upper.shape, upper.dtype),
             jax.ShapeDtypeStruct(lower.shape, lower.dtype),
         ),
-        in_specs=[
-            pl.BlockSpec(memory_space=pltpu.SMEM),
-            pl.BlockSpec((rows, 2, piece, width), lambda p: (0, p, 0, 0)),
-            pl.BlockSpec((1, piece, order), lambda p: (p, 0, 0)),
-            part(upper),
-            part(lower),
+        in_specs=[pl.BlockSpec(memory_space=pltpu.SMEM), vmem, vmem, vmem, vmem],
+        out_specs=(anywhere, anywhere, anywhere),
+        scratch_shapes=[
+            pltpu.VMEM(initial.shape, initial.dtype),
+            pltpu.SemaphoreType.DMA((parents + 2,)),
         ],
-        out_specs=(
-            pl.BlockSpec((1, piece, order), lambda p: (p, 0, 0)),
-            part(upper),
-            part(lower),
-        ),
-        compiler_params=pltpu.CompilerParams(vmem_limit_bytes=58 * MIB),
+        compiler_params=pltpu.CompilerParams(vmem_limit_bytes=8 * MIB),
     )(place, arrived, initial, upper, lower)
 
 

time: 192 us -> 189 us (0.984)
  Pallas kernels: 189 us -> 185 us
    pallas_call x1, Pallas kernels: 8.95 us -> 4.94 us  [assemble(): pl.pallas_call(assemble_kernel, out_shape=(jax.ShapeDtypeStruct(initial.s...]
where the time goes in v6:
time: 189 us; the launch traced here: 186 us
  Pallas kernels  185 us (98%)
    pallas_call x1, Pallas kernels, factor_update(): pl.pallas_call(factor_update_exchange, out_shape=(jax.ShapeDtypeStruct((w...  180 us
    pallas_call x1, Pallas kernels, assemble(): pl.pallas_call(assemble_kernel, out_shape=(jax.ShapeDtypeStruct(initial.s...  4.94 us

profile of v6, /device:TPU:15, one launch (start us, length us, event | category | flops | bytes accessed | tf_op | source)
XLA Modules:
  0.0 186.0 jit_solution(13688963569409278059)
XLA Ops:
  0.6 0.0 copy-start
  0.6 180.3 %shard_map.103 = (bf16[448,1024]{1,0:T(8,128)(2,1)S(1)}, bf16[512,1024]{1,0:T(8,128)(2,1)S(1)}, bf16[128,64,512]{2,1,0:T(8,128)(2,1)S(1)}, s32[16,128]{1,0:T(8,128)S(1)}) custom-call(s32[8,64]{1,0:T(8,128)} %slot_rows_in.1, s32[8,64]{1,0:T(8,128)} %slot_rows_in.1, s32[8,56]{1,0:T(8,128)} %parent_map_in.1, s32[1,1024]{1,0:T(1,128)} %order_in.1, ...), custom_call_target="tpu_custom_call" | custom-call | tf_op jit(solution)/shard_map/pallas_call | solution.py:362
  180.9 0.0 copy-done
  180.9 4.9 %shard_map.104 = (bf16[4,64,8192]{2,1,0:T(8,128)(2,1)}, bf16[448,1024]{1,0:T(8,128)(2,1)}, bf16[512,1024]{1,0:T(8,128)(2,1)}) custom-call(s32[16,128]{1,0:T(8,128)S(1)} %get-tuple-element.10.place, bf16[16,8,64,512]{3,2,1,0:T(8,128)(2,1)S(1)} %bitcast.6, bf16[4,64,8192]{2,1,0:T(8,128)(2,1)S(1)} %copy-done, bf16[448,1024]{1,0:T(8,128)(2,1)S(1)} %get-tuple-element.12.upper, ...), custom_call_target="tpu_custom_call" | custom-call | tf_op jit(solution)/shard_map/pallas_call | solution.py:470
Async XLA Ops:
  0.6 180.3 %copy-start = (bf16[4,64,8192]{2,1,0:T(8,128)(2,1)S(1)}, bf16[4,64,8192]{2,1,0:T(8,128)(2,1)}, u32[]{:S(2)}) copy-start(bf16[4,64,8192]{2,1,0:T(8,128)(2,1)} %initial.1) | copy-start | bytes 12582916

commit v7 on v6

--- a/solution.py
+++ b/solution.py
@@ -314,7 +314,7 @@
         spread[other] = jnp.where(at >= 0, value, jnp.zeros_like(value))
 
     def push(number, carry):
-        other = partner(lax.rem(number * 109, devices))
+        other = partner(lax.rem(number * 101, devices))
         to = other[0] * 8 + other[1]
         fill(to)
         pltpu.make_async_remote_copy(

time: 189 us -> 188 us (level)
  no operation moved by 1% of the time
where the time goes in v7:
time: 188 us; the launch traced here: 185 us
  Pallas kernels  184 us (98%)
    pallas_call x1, Pallas kernels, factor_update(): pl.pallas_call(factor_update_exchange, out_shape=(jax.ShapeDtypeStruct((w...  179 us
    pallas_call x1, Pallas kernels, assemble(): pl.pallas_call(assemble_kernel, out_shape=(jax.ShapeDtypeStruct(initial.s...  4.94 us

profile of v7, /device:TPU:15, one launch (start us, length us, event | category | flops | bytes accessed | tf_op | source)
XLA Modules:
  0.0 185.0 jit_solution(1587674947459575326)
XLA Ops:
  0.6 0.0 copy-start
  0.6 179.2 %shard_map.103 = (bf16[448,1024]{1,0:T(8,128)(2,1)S(1)}, bf16[512,1024]{1,0:T(8,128)(2,1)S(1)}, bf16[128,64,512]{2,1,0:T(8,128)(2,1)S(1)}, s32[16,128]{1,0:T(8,128)S(1)}) custom-call(s32[8,64]{1,0:T(8,128)} %slot_rows_in.1, s32[8,64]{1,0:T(8,128)} %slot_rows_in.1, s32[8,56]{1,0:T(8,128)} %parent_map_in.1, s32[1,1024]{1,0:T(1,128)} %order_in.1, ...), custom_call_target="tpu_custom_call" | custom-call | tf_op jit(solution)/shard_map/pallas_call | solution.py:362
  179.8 0.0 copy-done
  179.9 4.9 %shard_map.104 = (bf16[4,64,8192]{2,1,0:T(8,128)(2,1)}, bf16[448,1024]{1,0:T(8,128)(2,1)}, bf16[512,1024]{1,0:T(8,128)(2,1)}) custom-call(s32[16,128]{1,0:T(8,128)S(1)} %get-tuple-element.10.place, bf16[16,8,64,512]{3,2,1,0:T(8,128)(2,1)S(1)} %bitcast.6, bf16[4,64,8192]{2,1,0:T(8,128)(2,1)S(1)} %copy-done, bf16[448,1024]{1,0:T(8,128)(2,1)S(1)} %get-tuple-element.12.upper, ...), custom_call_target="tpu_custom_call" | custom-call | tf_op jit(solution)/shard_map/pallas_call | solution.py:470
Async XLA Ops:
  0.6 179.2 %copy-start = (bf16[4,64,8192]{2,1,0:T(8,128)(2,1)S(1)}, bf16[4,64,8192]{2,1,0:T(8,128)(2,1)}, u32[]{:S(2)}) copy-start(bf16[4,64,8192]{2,1,0:T(8,128)(2,1)} %initial.1) | copy-start | bytes 12582916

commit v8 on v7

--- a/solution.py
+++ b/solution.py
@@ -429,8 +429,8 @@
     block_rows = 128
     slots = arrived.shape[3] // block_rows
     stores = [
-        pltpu.make_async_copy(upper, upper_out, store_sem.at[parents]),
-        pltpu.make_async_copy(lower, lower_out, store_sem.at[parents + 1]),
+        pltpu.make_async_copy(upper, upper_out, store_sem.at[parents * 2]),
+        pltpu.make_async_copy(lower, lower_out, store_sem.at[parents * 2 + 1]),
     ]
     for copy in stores:
         copy.start()
@@ -455,10 +455,17 @@
                 total[parent, :, lanes] = (first.astype(jnp.float32) + both).astype(jnp.bfloat16)
             return carry
 
-        lax.fori_loop(0, order // block_rows // together, some, 0, unroll=2)
-        store = pltpu.make_async_copy(total.at[parent], out.at[parent], store_sem.at[parent])
-        store.start()
-        stores.append(store)
+        steps = order // block_rows // together // 2
+        for half in range(2):
+            lax.fori_loop(half * steps, (half + 1) * steps, some, 0, unroll=2)
+            span = pl.ds(half * (order // 2), order // 2)
+            store = pltpu.make_async_copy(
+                total.at[parent, :, span],
+                out.at[parent, :, span],
+                store_sem.at[parent * 2 + half],
+            )
+            store.start()
+            stores.append(store)
     for copy in stores:
         copy.wait()
 
@@ -478,7 +485,7 @@
         out_specs=(anywhere, anywhere, anywhere),
         scratch_shapes=[
             pltpu.VMEM(initial.shape, initial.dtype),
-            pltpu.SemaphoreType.DMA((parents + 2,)),
+            pltpu.SemaphoreType.DMA((parents * 2 + 2,)),
         ],
         compiler_params=pltpu.CompilerParams(vmem_limit_bytes=8 * MIB),
     )(place, arrived, initial, upper, lower)

time: 188 us -> 188 us (level)
  no operation moved by 1% of the time
where the time goes in v8:
time: 188 us; the launch traced here: 185 us
  Pallas kernels  184 us (98%)
    pallas_call x1, Pallas kernels, factor_update(): pl.pallas_call(factor_update_exchange, out_shape=(jax.ShapeDtypeStruct((w...  179 us
    pallas_call x1, Pallas kernels, assemble(): pl.pallas_call(assemble_kernel, out_shape=(jax.ShapeDtypeStruct(initial.s...  4.81 us

profile of v8, /device:TPU:15, one launch (start us, length us, event | category | flops | bytes accessed | tf_op | source)
XLA Modules:
  0.0 184.8 jit_solution(648002636835836850)
XLA Ops:
  0.6 0.0 copy-start
  0.6 179.2 %shard_map.103 = (bf16[448,1024]{1,0:T(8,128)(2,1)S(1)}, bf16[512,1024]{1,0:T(8,128)(2,1)S(1)}, bf16[128,64,512]{2,1,0:T(8,128)(2,1)S(1)}, s32[16,128]{1,0:T(8,128)S(1)}) custom-call(s32[8,64]{1,0:T(8,128)} %slot_rows_in.1, s32[8,64]{1,0:T(8,128)} %slot_rows_in.1, s32[8,56]{1,0:T(8,128)} %parent_map_in.1, s32[1,1024]{1,0:T(1,128)} %order_in.1, ...), custom_call_target="tpu_custom_call" | custom-call | tf_op jit(solution)/shard_map/pallas_call | solution.py:362
  179.8 0.0 copy-done
  179.9 4.8 %shard_map.104 = (bf16[4,64,8192]{2,1,0:T(8,128)(2,1)}, bf16[448,1024]{1,0:T(8,128)(2,1)}, bf16[512,1024]{1,0:T(8,128)(2,1)}) custom-call(s32[16,128]{1,0:T(8,128)S(1)} %get-tuple-element.10.place, bf16[16,8,64,512]{3,2,1,0:T(8,128)(2,1)S(1)} %bitcast.6, bf16[4,64,8192]{2,1,0:T(8,128)(2,1)S(1)} %copy-done, bf16[448,1024]{1,0:T(8,128)(2,1)S(1)} %get-tuple-element.12.upper, ...), custom_call_target="tpu_custom_call" | custom-call | tf_op jit(solution)/shard_map/pallas_call | solution.py:477
Async XLA Ops:
  0.6 179.2 %copy-start = (bf16[4,64,8192]{2,1,0:T(8,128)(2,1)S(1)}, bf16[4,64,8192]{2,1,0:T(8,128)(2,1)}, u32[]{:S(2)}) copy-start(bf16[4,64,8192]{2,1,0:T(8,128)(2,1)} %initial.1) | copy-start | bytes 12582916
